TPU v7x, 32 devices: a whole 2x2x4 slice. The times are simulated.
32 devices in a mesh: dp: 4 (over y, x), vocab: 8 (over z, core).
Axes of the slice: x: 2, y: 2, z: 4, core: 2. Of those that a mesh axis runs over, the one named last changes fastest.
Arguments:
- hidden: bfloat16 [512, 3072], P('dp')
- head: bfloat16 [4, 8192, 3072], P('dp', 'vocab')
- teacher: bfloat16 [512, 32768], P('dp', 'vocab')
- shard_order: int32 [8], replicated, may hold values from 0 to 7, each once
- loss_weight: float32 [512], replicated, may hold values from 256 to 2048
Outputs:
- head_grad: bfloat16 [4, 8192, 3072], P('dp', 'vocab')
- divergence: float32 [512], replicated
Inputs may be any that keep to these rules, and one draw needn't show every extreme that they name: `shard_order`: each block number appears once.
All inputs are finite; a program needn't handle non-finite values.
Results may differ from a plain program's by a relative error of at most 0.0048.
Values may be sent and summed in bfloat16 or wider, within the bound.
No kernel may reach another device: no remote copies, remote signals or barrier semaphores. Data moves between devices by JAX's collectives and lax.ppermute only.
A program may use at most 128 MiB of HBM per device.

v0:
```python
import functools
import itertools

import jax
import jax.numpy as jnp
import numpy as np
from jax import lax
from jax.experimental import pallas as pl
from jax.experimental.pallas import tpu as pltpu
from jax.sharding import PartitionSpec as P

MIB = 1024 * 1024
LOWEST = float(np.finfo(np.float32).min)
NO_PLAN = 2**30


def xor_permute(x, axis, k):
    size = lax.axis_size(axis)
    return lax.ppermute(x, axis, [(i, i ^ k) for i in range(size)])


def device_count():
    return lax.axis_size("dp") * lax.axis_size("vocab")


def exchange(copies):
    return lax.all_to_all(copies, ("dp", "vocab"), split_axis=0, concat_axis=0, tiled=True)


def log_sum_exp(parts, axis):
    top = jnp.max(parts, axis=axis, keepdims=True)
    total = jnp.sum(jnp.exp(parts - top), axis=axis, keepdims=True)
    return jnp.squeeze(top + jnp.log(total), axis)


def combine_stats(parts, tokens):
    n_dp, n_vocab = lax.axis_size("dp"), lax.axis_size("vocab")
    student = log_sum_exp(parts[:, 0, :tokens], 0)
    target = log_sum_exp(parts[:, 0, tokens:].reshape(n_dp, n_vocab, tokens // n_dp), 1)
    return student, target.reshape(tokens)


def place(rows):
    return lambda k: pl.multiple_of((lax.axis_index("dp") ^ k) * rows, rows)


def student_kernel(n_chunks, *refs):
    chunk_refs = refs[:n_chunks]
    head_ref, teacher_ref, out_ref, hid_out_ref, stats_ref = refs[n_chunks : n_chunks + 5]
    hid_ref, rows_ref, logits_ref, scores_ref, top_ref, sum_ref, stat_ref = refs[n_chunks + 5 : -4]
    chunk_sems, head_sems, out_sems, sems = refs[-4:]
    tokens, rows = scores_ref.shape
    own = teacher_ref.shape[0]
    block = min(256, rows)
    blocks = rows // block

    def head_copy(i):
        here = pl.ds(pl.multiple_of(i * block, block), block)
        return pltpu.make_async_copy(head_ref.at[0, here], rows_ref.at[here], head_sems.at[i])

    def out_copy(i):
        here = pl.ds(pl.multiple_of(i * block, block), block)
        return pltpu.make_async_copy(scores_ref.at[:, here], out_ref.at[:, here], out_sems.at[i])

    teacher_copy = pltpu.make_async_copy(teacher_ref, logits_ref, sems.at[0])
    hid_copy = pltpu.make_async_copy(hid_ref, hid_out_ref, sems.at[1])
    copies = []
    for k, ref in enumerate(chunk_refs):
        copies.append(
            pltpu.make_async_copy(ref, hid_ref.at[k * own : (k + 1) * own], chunk_sems.at[k])
        )
    teacher_copy.start()
    for copy in copies:
        copy.start()
    for i in range(blocks):
        head_copy(i).start()

    top_ref[...] = jnp.full(top_ref.shape, LOWEST, jnp.float32)
    sum_ref[...] = jnp.zeros(sum_ref.shape, jnp.float32)
    teacher_copy.wait()
    values = logits_ref[...].astype(jnp.float32)
    top = jnp.max(values, axis=1, keepdims=True)
    total = jnp.sum(jnp.exp(values - top), axis=1, keepdims=True)
    stat = jnp.transpose(jnp.broadcast_to(top + jnp.log(total), (own, 128)))[0:1]
    stats_ref[:, :, tokens:] = jnp.broadcast_to(stat[None], (stats_ref.shape[0], 1, own))
    for copy in copies:
        copy.wait()
    hid_copy.start()

    def step(i, carry):
        columns = pl.ds(pl.multiple_of(i * block, block), block)
        head_copy(i).wait()
        part = min(256, tokens)
        for first in range(0, tokens, part):
            here = slice(first, first + part)
            scores = lax.dot_general(
                hid_ref[here],
                rows_ref[columns],
                (((1,), (1,)), ((), ())),
                preferred_element_type=jnp.float32,
            )
            scores_ref[here, columns] = scores
            old = top_ref[here]
            top = jnp.maximum(old, jnp.max(scores, axis=1, keepdims=True))
            total = jnp.sum(jnp.exp(scores - top), axis=1, keepdims=True)
            top_ref[here] = top
            sum_ref[here] = sum_ref[here] * jnp.exp(old - top) + total
        out_copy(i).start()
        return carry

    lax.fori_loop(0, blocks, step, 0)
    at = place(own)
    for k in range(n_chunks):
        here = slice(k * own, (k + 1) * own)
        stat = top_ref[here] + jnp.log(sum_ref[here])
        stat_ref[pl.ds(at(k), own)] = jnp.broadcast_to(stat, (own, 128))
    stat = jnp.transpose(stat_ref[...])[0:1]
    stats_ref[:, :, :tokens] = jnp.broadcast_to(stat[None], (stats_ref.shape[0], 1, tokens))
    for i in range(blocks):
        out_copy(i).wait()
    hid_copy.wait()


def student_call(chunks, head, teacher, tokens):
    _, rows, depth = head.shape
    blocks = rows // min(256, rows)
    in_hbm = pl.BlockSpec(memory_space=pltpu.HBM)
    return pl.pallas_call(
        functools.partial(student_kernel, len(chunks)),
        in_specs=[in_hbm] * (len(chunks) + 2),
        out_specs=[in_hbm, in_hbm, pl.BlockSpec(memory_space=pltpu.VMEM)],
        out_shape=[
            jax.ShapeDtypeStruct((tokens, rows), jnp.float32),
            jax.ShapeDtypeStruct((tokens, depth), jnp.bfloat16),
            jax.ShapeDtypeStruct((device_count(), 1, tokens + teacher.shape[0]), jnp.float32),
        ],
        scratch_shapes=[
            pltpu.VMEM((tokens, depth), jnp.bfloat16),
            pltpu.VMEM((rows, depth), jnp.bfloat16),
            pltpu.VMEM(teacher.shape, jnp.bfloat16),
            pltpu.VMEM((tokens, rows), jnp.float32),
            pltpu.VMEM((tokens, 1), jnp.float32),
            pltpu.VMEM((tokens, 1), jnp.float32),
            pltpu.VMEM((tokens, 128), jnp.float32),
            pltpu.SemaphoreType.DMA((len(chunks),)),
            pltpu.SemaphoreType.DMA((blocks,)),
            pltpu.SemaphoreType.DMA((blocks,)),
            pltpu.SemaphoreType.DMA((2,)),
        ],
        compiler_params=pltpu.CompilerParams(vmem_limit_bytes=60 * MIB),
        cost_estimate=pl.CostEstimate(
            flops=2 * tokens * rows * depth,
            bytes_accessed=2 * rows * depth + 2 * tokens * depth + 4 * tokens * rows,
            transcendentals=tokens * rows,
        ),
        name="student",
    )(*chunks, head, teacher)


def logit_grad_kernel(
    flags_ref, mine_ref, got_ref, scores_ref, row_s_ref, row_t_ref, weight_ref, grad_ref, cross_ref, col_ref
):
    step, last = pl.program_id(0), pl.num_programs(0) - 1
    rows = scores_ref.shape[0]
    tokens = col_ref.shape[0]
    half = rows // 2
    at = place(rows)(step)

    @pl.when(step == 0)
    def _():
        line = lax.broadcasted_iota(jnp.int32, (128, tokens), 0)
        col_ref[...] = jnp.transpose(
            jnp.where(line == 0, row_s_ref[...], jnp.where(line == 1, row_t_ref[...], weight_ref[...]))
        )

    keep = flags_ref[1] != 0
    for first in (0, half):
        part = slice(first, first + half)
        here = pl.ds(pl.multiple_of(at + first, half), half)
        cols = col_ref[here]
        student = scores_ref[part]
        target = jnp.where(keep, mine_ref[0, part], got_ref[0, part]).astype(jnp.float32)
        prob_s = jnp.exp(student - cols[:, 0:1])
        prob_t = jnp.exp(target - cols[:, 1:2])
        cross = jnp.sum(prob_t * (target - student), axis=1, keepdims=True)
        grad_ref[part] = (cols[:, 2:3] * (prob_s - prob_t)).astype(jnp.bfloat16)
        col_ref[here] = jnp.broadcast_to(cross, (half, 128))

    @pl.when(step == last)
    def _():
        cross = jnp.transpose(col_ref[...])[0:1]
        cross_ref[...] = jnp.broadcast_to(cross[None], cross_ref.shape)


def logit_grad_call(flags, mine, got, scores, total_s, total_t, weight):
    n_dp, part, rows = mine.shape
    tokens = n_dp * part
    cross = (device_count(), 1, tokens)
    whole_row = pl.BlockSpec((1, tokens), lambda k: (0, 0))
    return pl.pallas_call(
        logit_grad_kernel,
        grid=(n_dp,),
        in_specs=[
            pl.BlockSpec(memory_space=pltpu.SMEM),
            pl.BlockSpec((1, part, rows), lambda k: (k, 0, 0)),
            pl.BlockSpec((1, part, rows), lambda k: (k, 0, 0)),
            pl.BlockSpec((part, rows), lambda k: (k, 0)),
            whole_row,
            whole_row,
            whole_row,
        ],
        out_specs=[
            pl.BlockSpec((part, rows), lambda k: (k, 0)),
            pl.BlockSpec(cross, lambda k: (0, 0, 0)),
        ],
        out_shape=[
            jax.ShapeDtypeStruct((tokens, rows), jnp.bfloat16),
            jax.ShapeDtypeStruct(cross, jnp.float32),
        ],
        scratch_shapes=[pltpu.VMEM((tokens, 128), jnp.float32)],
        compiler_params=pltpu.CompilerParams(vmem_limit_bytes=24 * MIB),
        cost_estimate=pl.CostEstimate(
            flops=8 * tokens * rows, bytes_accessed=8 * tokens * rows, transcendentals=2 * tokens * rows
        ),
        name="logit_grad",
    )(flags, mine, got, scores, total_s[None], total_t[None], weight[None])


def head_grad_kernel(grad_ref, hid_ref, out_ref):
    out_ref[0] = lax.dot_general(
        grad_ref[...], hid_ref[...], (((0,), (0,)), ((), ())), preferred_element_type=jnp.float32
    ).astype(jnp.bfloat16)


def head_grad_call(logit_grad, hid):
    tokens, rows = logit_grad.shape
    depth = hid.shape[1]
    block = min(256, rows)
    return pl.pallas_call(
        head_grad_kernel,
        grid=(rows // block,),
        in_specs=[
            pl.BlockSpec((tokens, block), lambda i: (0, i)),
            pl.BlockSpec((tokens, depth), lambda i: (0, 0)),
        ],
        out_specs=pl.BlockSpec((1, block, depth), lambda i: (0, i, 0)),
        out_shape=jax.ShapeDtypeStruct((1, rows, depth), jnp.bfloat16),
        compiler_params=pltpu.CompilerParams(vmem_limit_bytes=60 * MIB),
        cost_estimate=pl.CostEstimate(
            flops=2 * tokens * rows * depth,
            bytes_accessed=2 * rows * depth + 2 * tokens * depth,
            transcendentals=0,
        ),
        name="head_grad",
    )(logit_grad, hid)


def chip_plans(n):
    def load(pair):
        ups = [sum(z < c <= p[z] for p in pair for z in range(n)) for c in range(1, n)]
        return max(ups), sum(ups)

    best = {}
    perms = list(itertools.permutations(range(n)))
    for pair in itertools.combinations_with_replacement(perms, 2):
        code = sum(3 ** (n * z + p[z]) for p in pair for z in range(n))
        if code not in best or load(pair) < load(best[code]):
            best[code] = pair
    return sorted(best.items())


def plan_tables(plans, n):
    codes = [code for code, _ in plans]
    keys = [
        (i << 8) | sum(first[z] << (2 * z) for z in range(n)) for i, (_, (first, _)) in enumerate(plans)
    ]
    pad = -len(codes) % 1024
    codes = np.array(codes + [-1] * pad, np.int32).reshape(-1, 128)
    keys = np.array(keys + [NO_PLAN] * pad, np.int32).reshape(-1, 128)
    return codes, keys


def plan_kernel(n_chips, order_ref, codes_ref, keys_ref, number_ref, flags_ref):
    chip = lax.axis_index("vocab") // 2
    code = jnp.int32(0)
    for block in range(2 * n_chips):
        dest = order_ref[block] // 2
        power = jnp.int32(0)
        for d in range(n_chips):
            power = jnp.where(dest == d, 3 ** (n_chips * (block // 2) + d), power)
        code = code + power
    key = jnp.min(jnp.where(codes_ref[...] == code, keys_ref[...], NO_PLAN))
    sends = jnp.int32(0)
    arrives = jnp.int32(0)
    for z in range(n_chips):
        goes = (key >> (2 * z)) & 3
        source = jnp.where(order_ref[2 * z] // 2 == goes, 0, 1)
        meant = jnp.where(source == 0, order_ref[2 * z], order_ref[2 * z + 1]) & 1
        sends = jnp.where(chip == z, source, sends)
        arrives = jnp.where(goes == chip, meant, arrives)
    number_ref[0] = key >> 8
    flags_ref[0] = 1 - sends
    flags_ref[1] = 1 - arrives


def plan_chips(shard_order, plans, n_chips):
    codes, keys = plan_tables(plans, n_chips)
    in_smem = pl.BlockSpec(memory_space=pltpu.SMEM)
    in_vmem = pl.BlockSpec(memory_space=pltpu.VMEM)
    return pl.pallas_call(
        functools.partial(plan_kernel, n_chips),
        in_specs=[in_smem, in_vmem, in_vmem],
        out_specs=[in_smem] * 2,
        out_shape=[jax.ShapeDtypeStruct((n,), jnp.int32) for n in (1, 2)],
        compiler_params=pltpu.CompilerParams(vmem_limit_bytes=60 * MIB),
        name="plan",
    )(shard_order, jnp.asarray(codes), jnp.asarray(keys))


def pick_kernel(flags_ref, mine_ref, other_ref, out_ref):
    dp = lax.axis_index("dp")
    n_dp, _, cols = out_ref.shape
    own = flags_ref[0] != 0
    for k in range(n_dp):
        here = pl.ds(pl.multiple_of((dp ^ k) * cols, cols), cols)
        out_ref[k] = jnp.where(own, mine_ref[:, here], other_ref[:, here])


def pick_call(flags, mine, other):
    n_dp = lax.axis_size("dp")
    shape = (n_dp, mine.shape[0], mine.shape[1] // n_dp)
    in_vmem = pl.BlockSpec(memory_space=pltpu.VMEM)
    return pl.pallas_call(
        pick_kernel,
        in_specs=[pl.BlockSpec(memory_space=pltpu.SMEM), in_vmem, in_vmem],
        out_specs=in_vmem,
        out_shape=jax.ShapeDtypeStruct(shape, jnp.bfloat16),
        compiler_params=pltpu.CompilerParams(vmem_limit_bytes=24 * MIB),
        name="pick",
    )(flags, mine, other)


def join_kernel(*refs):
    for k, ref in enumerate(refs[:-1]):
        refs[-1][k] = ref[...]


def join_call(pieces):
    in_vmem = pl.BlockSpec(memory_space=pltpu.VMEM)
    return pl.pallas_call(
        join_kernel,
        in_specs=[in_vmem] * len(pieces),
        out_specs=in_vmem,
        out_shape=jax.ShapeDtypeStruct((len(pieces), *pieces[0].shape), jnp.bfloat16),
        compiler_params=pltpu.CompilerParams(vmem_limit_bytes=24 * MIB),
        name="join",
    )(*pieces)


def over_dp(pieces):
    return [pieces[0]] + [xor_permute(pieces[k], "dp", k) for k in range(1, len(pieces))]


def wide_block(teacher, shard_order):
    token_rows = teacher.shape[0]
    n_vocab = lax.axis_size("vocab")
    piece_cols = teacher.shape[1] // n_vocab
    split_view = teacher.reshape(token_rows, n_vocab, piece_cols)
    spread_view = lax.all_to_all(split_view, "vocab", split_axis=1, concat_axis=1, tiled=True)
    ordinal = jnp.arange(n_vocab, dtype=jnp.int32)
    matches = (shard_order[None, :] == ordinal[:, None]).astype(jnp.int32)
    inverse = jnp.sum(matches * ordinal[None, :], axis=1)
    sorted_view = jnp.take(spread_view, inverse, axis=1)
    return lax.all_to_all(sorted_view, "vocab", split_axis=1, concat_axis=1, tiled=True).reshape(
        token_rows, n_vocab * piece_cols
    )


def on_device(hidden, head, teacher, shard_order, loss_weight):
    n_dp, n_vocab = lax.axis_size("dp"), lax.axis_size("vocab")
    n_chips = n_vocab // 2
    tokens = hidden.shape[0] * n_dp

    if n_chips <= 4:
        other = xor_permute(teacher, "vocab", 1)
        plans = chip_plans(n_chips)
        number, flags = plan_chips(shard_order, plans, n_chips)
        chunks = [hidden] + [xor_permute(hidden, "dp", k) for k in range(1, n_dp)]

        def over_chips(x, pair):
            pairs = [(2 * z + c, 2 * pair[c][z] + c) for z in range(n_chips) for c in range(2)]
            return lax.ppermute(x, "vocab", pairs)

        arrived = lax.switch(
            number[0],
            [functools.partial(over_chips, pair=pair) for _, pair in plans],
            pick_call(flags, teacher, other),
        )
        chunks, arrived = lax.optimization_barrier((chunks, arrived))
        pieces = over_dp([arrived[k] for k in range(n_dp)])
        student, hid, stats = student_call(chunks, head, teacher, tokens)
        pieces, stats = lax.optimization_barrier((pieces, stats))
        mine = join_call(pieces)
        got = xor_permute(mine, "vocab", 1)
    else:
        chunks = [hidden] + [xor_permute(hidden, "dp", k) for k in range(1, n_dp)]
        student, hid, stats = student_call(chunks, head, teacher, tokens)
        block = wide_block(teacher, shard_order)
        cols, dp = block.shape[1] // n_dp, lax.axis_index("dp")
        mine = jnp.stack(
            over_dp([lax.dynamic_slice_in_dim(block, (dp ^ k) * cols, cols, 1) for k in range(n_dp)])
        )
        flags, got = jnp.ones((2,), jnp.int32), mine

    total_s, total_t = combine_stats(exchange(stats), tokens)
    logit_grad, cross = logit_grad_call(flags, mine, got, student, total_s, total_t, loss_weight)
    head_grad = head_grad_call(logit_grad, hid)
    divergence = jnp.sum(exchange(cross), axis=(0, 1)) - total_t + total_s
    return head_grad, divergence


def solution(mesh):
    in_specs = (P("dp", None), P("dp", "vocab", None), P("dp", "vocab"), P(), P())
    out_specs = (P("dp", "vocab", None), P())
    return jax.shard_map(
        on_device, mesh=mesh, in_specs=in_specs, out_specs=out_specs, check_vma=False
    )
```

profile of v0, /device:TPU:0, one launch (start us, length us, event | category | flops | bytes accessed | tf_op | source)
XLA Modules:
  0.0 87.2 jit_solution(4411277062273991524)
XLA Ops:
  0.6 0.5 collective-permute-start.285
  1.1 2.6 %collective-permute-start.283 = (bf16[128,3072]{1,0:T(8,128)(2,1)}, bf16[128,3072]{1,0:T(8,128)(2,1)S(1)}, u32[]{:S(2)}, u32[]{:S(2)}) collective-permute-start(bf16[128,3072]{1,0:T(8,128)(2,1)} %refs_0_), channel_id=1, source_target_pairs={{0,16},{8,24},{16,0},{24,8},{1,17},{9,25},{17,1},{25,9},{2,18},{10... | collective-permute-start | bytes 2359304 | tf_op jit(solution)/shard_map/ppermute | solution.py:19
  3.7 1.5 %collective-permute-start.282 = (bf16[128,3072]{1,0:T(8,128)(2,1)}, bf16[128,3072]{1,0:T(8,128)(2,1)S(1)}, u32[]{:S(2)}, u32[]{:S(2)}) collective-permute-start(bf16[128,3072]{1,0:T(8,128)(2,1)} %refs_0_), channel_id=1, source_target_pairs={{0,8},{8,0},{16,24},{24,16},{1,9},{9,1},{17,25},{25,17},{2,10},{10... | collective-permute-start | bytes 2359304 | tf_op jit(solution)/shard_map/ppermute | solution.py:19
  5.2 0.1 collective-permute-start.284
  5.3 1.5 %plan.1 = (s32[1]{0:T(128)}, s32[2]{0:T(128)}) custom-call(s32[8]{0:T(128)} %order_ref.1, s32[8,128]{1,0:T(8,128)} %constant.14.clone.codes_ref, s32[8,128]{1,0:T(8,128)} %constant.15.clone.keys_ref), custom_call_target="tpu_custom_call" | custom-call | tf_op jit(solution)/shard_map/plan/pallas_call | solution.py:310
  7.4 0.0 collective-permute-done.285.other_ref
  7.5 0.0 copy-start.1
  7.5 1.2 %copy-done.1 = bf16[128,4096]{1,0:T(8,128)(2,1)S(1)} copy-done((bf16[128,4096]{1,0:T(8,128)(2,1)S(1)}, bf16[128,4096]{1,0:T(8,128)(2,1)}, u32[]{:S(2)}) %copy-start.1) | copy-done | bytes 1048600
  8.7 0.0 copy-start.3
  8.7 0.6 copy-done.3
  9.3 0.7 pick.1
  10.0 34.3 %conditional.1 = (bf16[4,128,1024]{2,1,0:T(8,128)(2,1)}) conditional(s32[]{:T(128)} %bitcast, bf16[4,128,1024]{2,1,0:T(8,128)(2,1)S(1)} %pick.1, bf16[4,128,1024]{2,1,0:T(8,128)(2,1)S(1)} %pick.1, bf16[4,128,1024]{2,1,0:T(8,128)(2,1)S(1)} %pick.1, bf16[4,128,1024]{2,1,0:T(8,128)(2,1)S(1)} %pick.1, ...), branch_computations={%region_0.0_spmd, %region_1.0_spmd, %region_2.0_spmd, %region_3.0_... | conditional | bytes 4194352 | solution.py:394
  10.0 7.3 %collective-permute-start.117 = (bf16[4,128,1024]{2,1,0:T(8,128)(2,1)S(1)}, bf16[4,128,1024]{2,1,0:T(8,128)(2,1)}, u32[]{:S(2)}, u32[]{:S(2)}) collective-permute-start(bf16[4,128,1024]{2,1,0:T(8,128)(2,1)S(1)} %param.117), channel_id=1, source_target_pairs={{0,2},{1,7},{2,6},{3,1},{4,0},{5,5},{6,4},{7,3},{8,10},{9,15},{10,... | collective-permute-start | bytes 3145736 | tf_op jit(solution)/shard_map/cond/branch_117_fun/ppermute | solution.py:392
  17.3 26.9 %collective-permute-done.117 = bf16[4,128,1024]{2,1,0:T(8,128)(2,1)} collective-permute-done((bf16[4,128,1024]{2,1,0:T(8,128)(2,1)S(1)}, bf16[4,128,1024]{2,1,0:T(8,128)(2,1)}, u32[]{:S(2)}, u32[]{:S(2)}) %collective-permute-start.117) | collective-permute-done | bytes 1048608 | tf_op jit(solution)/shard_map/cond/branch_117_fun/ppermute | solution.py:392
  44.2 0.0 collective-permute-done.283.refs_2_
  44.2 0.0 copy-start.6
  44.2 0.0 collective-permute-done.282.refs_1_
  44.2 0.0 copy-start.7
  44.3 0.0 collective-permute-done.284.refs_3_
  44.3 1.8 %slice_bitcast_fusion = (bf16[128,1024]{1,0:T(8,128)(2,1)S(1)}, bf16[128,1024]{1,0:T(8,128)(2,1)S(1)}, bf16[128,1024]{1,0:T(8,128)(2,1)S(1)}, bf16[128,1024]{1,0:T(8,128)(2,1)S(1)}) fusion(bf16[4,128,1024]{2,1,0:T(8,128)(2,1)} %get-tuple-element.607), kind=kLoop, calls=%fused_computation | loop fusion | bytes 2097152 | tf_op jit(solution)/shard_map/squeeze | solution.py:400
  46.1 2.5 %collective-permute-start.288 = (bf16[128,1024]{1,0:T(8,128)(2,1)S(1)}, bf16[128,1024]{1,0:T(8,128)(2,1)S(1)}, u32[]{:S(2)}, u32[]{:S(2)}) collective-permute-start(bf16[128,1024]{1,0:T(8,128)(2,1)S(1)} %get-tuple-element.601), channel_id=1, source_target_pairs={{0,24},{8,16},{16,8},{24,0},{1,25},{9,17},{17,9},{25,1},{2,26},{10... | collective-permute-start | bytes 786440 | tf_op jit(solution)/shard_map/ppermute | solution.py:19
  48.5 0.5 collective-permute-start.287
  49.1 0.0 copy-done.7
  49.1 0.0 copy-start.2
  49.1 0.0 copy-start.4
  49.1 0.6 collective-permute-start.286
  49.6 0.0 copy-done.6
  49.6 10.2 %student.1 = (f32[512,1024]{1,0:T(8,128)}, bf16[512,3072]{1,0:T(8,128)(2,1)}, f32[32,1,640]{2,1,0:T(1,128)}) custom-call(bf16[128,3072]{1,0:T(8,128)(2,1)} %refs_0_, bf16[128,3072]{1,0:T(8,128)(2,1)} %copy-done.7, bf16[128,3072]{1,0:T(8,128)(2,1)} %copy-done.6, bf16[128,3072]{1,0:T(8,128)(2,1)} %collective-permute-done.284.refs_3_, ...), custom_call_target="tpu_custom_call" | custom-call | flops 3221225472 | bytes 11534336 | tf_op jit(solution)/shard_map/student/pallas_call | solution.py:128
  59.9 0.0 collective-permute-done.288.refs_3_
  59.9 0.0 collective-permute-done.287.refs_2_
  59.9 0.0 collective-permute-done.286.refs_1_
  59.9 3.2 %all-to-all-start = ((f32[32,1,640]{2,1,0:T(1,128)}), f32[32,1,640]{2,1,0:T(1,128)S(1)}, u32[]{:S(2)}, u32[]{:S(2)}) async-start(f32[32,1,640]{2,1,0:T(1,128)} %get-tuple-element.597), calls=%async_computation | async-start | bytes 163840 | tf_op jit(solution)/shard_map/all_to_all | solution.py:27
  63.1 0.1 join.1.mine_ref
  63.2 0.3 collective-permute-start.289
  63.5 7.2 %all-to-all-done = f32[32,1,640]{2,1,0:T(1,128)S(1)} async-done(((f32[32,1,640]{2,1,0:T(1,128)}), f32[32,1,640]{2,1,0:T(1,128)S(1)}, u32[]{:S(2)}, u32[]{:S(2)}) %all-to-all-start) | async-done | bytes 81952 | tf_op jit(solution)/shard_map/all_to_all | solution.py:27
  70.8 0.1 fusion.5
  70.9 0.0 collective-permute-done.289.got_ref
  70.9 0.0 copy-done.2
  70.9 0.0 copy-done.4
  70.9 0.0 copy-start
  71.0 1.6 %copy-done = f32[512,1024]{1,0:T(8,128)S(1)} copy-done((f32[512,1024]{1,0:T(8,128)S(1)}, f32[512,1024]{1,0:T(8,128)}, u32[]{:S(2)}) %copy-start) | copy-done | bytes 2097176
  72.5 3.0 %logit_grad.1 = (bf16[512,1024]{1,0:T(8,128)(2,1)S(1)}, f32[32,1,512]{2,1,0:T(1,128)}) custom-call(s32[2]{0:T(128)S(1)} %copy-done.4, bf16[4,128,1024]{2,1,0:T(8,128)(2,1)S(1)} %join.1.mine_ref, bf16[4,128,1024]{2,1,0:T(8,128)(2,1)S(1)} %collective-permute-done.289.got_ref, f32[512,1024]{1,0:T(8,128)S(1)} %copy-done, f32[1,512]{1,0:T(1,128)S(1)} %bitcast.31, ...), custom_call_target="tpu_custom_call" | custom-call | flops 4194304 | bytes 4194304 | tf_op jit(solution)/shard_map/logit_grad/pallas_call | solution.py:200
  75.5 1.1 %copy-done.5 = bf16[512,1024]{1,0:T(8,128)(2,1)} copy-done((bf16[512,1024]{1,0:T(8,128)(2,1)}, bf16[512,1024]{1,0:T(8,128)(2,1)S(1)}, u32[]{:S(2)}) %copy-start.5) | copy-done | bytes 1048600
  76.6 2.5 %all-to-all-start.1 = ((f32[32,1,512]{2,1,0:T(1,128)}), f32[32,1,512]{2,1,0:T(1,128)S(1)}, u32[]{:S(2)}, u32[]{:S(2)}) async-start(f32[32,1,512]{2,1,0:T(1,128)} %get-tuple-element.600), calls=%async_computation.1 | async-start | bytes 131072 | tf_op jit(solution)/shard_map/all_to_all | solution.py:27
  79.1 7.5 %head_grad.1 = bf16[1,1024,3072]{2,1,0:T(8,128)(2,1)} custom-call(bf16[512,1024]{1,0:T(8,128)(2,1)} %copy-done.5, bf16[512,3072]{1,0:T(8,128)(2,1)} %get-tuple-element.599.hid_ref), custom_call_target="tpu_custom_call" | custom-call | flops 3221225472 | bytes 9437184 | tf_op jit(solution)/shard_map/head_grad/pallas_call | solution.py:239
  86.6 0.0 all-to-all-done.1
  86.6 0.1 reduce_sum.29
  86.6 0.6 fusion.4
  (7 shorter events, 0.1 us)
Async XLA Ops:
  0.6 6.8 %collective-permute-start.285 = (bf16[128,4096]{1,0:T(8,128)(2,1)}, bf16[128,4096]{1,0:T(8,128)(2,1)S(1)}, u32[]{:S(2)}, u32[]{:S(2)}) collective-permute-start(bf16[128,4096]{1,0:T(8,128)(2,1)} %refs_5_.1), channel_id=1, source_target_pairs={{0,1},{1,0},{2,3},{3,2},{4,5},{5,4},{6,7},{7,6},{8,9},{9,8},{10,11... | collective-permute-start | bytes 3145736 | tf_op jit(solution)/shard_map/ppermute | solution.py:19
  1.1 43.1 %collective-permute-start.283 = (bf16[128,3072]{1,0:T(8,128)(2,1)}, bf16[128,3072]{1,0:T(8,128)(2,1)S(1)}, u32[]{:S(2)}, u32[]{:S(2)}) collective-permute-start(bf16[128,3072]{1,0:T(8,128)(2,1)} %refs_0_), channel_id=1, source_target_pairs={{0,16},{8,24},{16,0},{24,8},{1,17},{9,25},{17,1},{25,9},{2,18},{10... | collective-permute-start | bytes 2359304 | tf_op jit(solution)/shard_map/ppermute | solution.py:19
  3.7 40.5 %collective-permute-start.282 = (bf16[128,3072]{1,0:T(8,128)(2,1)}, bf16[128,3072]{1,0:T(8,128)(2,1)S(1)}, u32[]{:S(2)}, u32[]{:S(2)}) collective-permute-start(bf16[128,3072]{1,0:T(8,128)(2,1)} %refs_0_), channel_id=1, source_target_pairs={{0,8},{8,0},{16,24},{24,16},{1,9},{9,1},{17,25},{25,17},{2,10},{10... | collective-permute-start | bytes 2359304 | tf_op jit(solution)/shard_map/ppermute | solution.py:19
  5.2 39.0 %collective-permute-start.284 = (bf16[128,3072]{1,0:T(8,128)(2,1)}, bf16[128,3072]{1,0:T(8,128)(2,1)}, u32[]{:S(2)}, u32[]{:S(2)}) collective-permute-start(bf16[128,3072]{1,0:T(8,128)(2,1)} %refs_0_), channel_id=1, source_target_pairs={{0,24},{8,16},{16,8},{24,0},{1,25},{9,17},{17,9},{25,1},{2,26},{10... | collective-permute-start | bytes 2359304 | tf_op jit(solution)/shard_map/ppermute | solution.py:19
  7.5 1.2 %copy-start.1 = (bf16[128,4096]{1,0:T(8,128)(2,1)S(1)}, bf16[128,4096]{1,0:T(8,128)(2,1)}, u32[]{:S(2)}) copy-start(bf16[128,4096]{1,0:T(8,128)(2,1)} %refs_5_.1) | copy-start | bytes 3145732
  8.7 0.6 copy-start.3
  10.0 34.2 %collective-permute-start.117 = (bf16[4,128,1024]{2,1,0:T(8,128)(2,1)S(1)}, bf16[4,128,1024]{2,1,0:T(8,128)(2,1)}, u32[]{:S(2)}, u32[]{:S(2)}) collective-permute-start(bf16[4,128,1024]{2,1,0:T(8,128)(2,1)S(1)} %param.117), channel_id=1, source_target_pairs={{0,2},{1,7},{2,6},{3,1},{4,0},{5,5},{6,4},{7,3},{8,10},{9,15},{10,... | collective-permute-start | bytes 3145736 | tf_op jit(solution)/shard_map/cond/branch_117_fun/ppermute | solution.py:392
  44.2 5.4 %copy-start.6 = (bf16[128,3072]{1,0:T(8,128)(2,1)}, bf16[128,3072]{1,0:T(8,128)(2,1)S(1)}, u32[]{:S(2)}) copy-start(bf16[128,3072]{1,0:T(8,128)(2,1)S(1)} %collective-permute-done.283.refs_2_) | copy-start | bytes 2359300
  44.2 4.8 %copy-start.7 = (bf16[128,3072]{1,0:T(8,128)(2,1)}, bf16[128,3072]{1,0:T(8,128)(2,1)S(1)}, u32[]{:S(2)}) copy-start(bf16[128,3072]{1,0:T(8,128)(2,1)S(1)} %collective-permute-done.282.refs_1_) | copy-start | bytes 2359300
  46.1 13.8 %collective-permute-start.288 = (bf16[128,1024]{1,0:T(8,128)(2,1)S(1)}, bf16[128,1024]{1,0:T(8,128)(2,1)S(1)}, u32[]{:S(2)}, u32[]{:S(2)}) collective-permute-start(bf16[128,1024]{1,0:T(8,128)(2,1)S(1)} %get-tuple-element.601), channel_id=1, source_target_pairs={{0,24},{8,16},{16,8},{24,0},{1,25},{9,17},{17,9},{25,1},{2,26},{10... | collective-permute-start | bytes 786440 | tf_op jit(solution)/shard_map/ppermute | solution.py:19
  48.5 11.4 %collective-permute-start.287 = (bf16[128,1024]{1,0:T(8,128)(2,1)S(1)}, bf16[128,1024]{1,0:T(8,128)(2,1)S(1)}, u32[]{:S(2)}, u32[]{:S(2)}) collective-permute-start(bf16[128,1024]{1,0:T(8,128)(2,1)S(1)} %get-tuple-element.602), channel_id=1, source_target_pairs={{0,16},{8,24},{16,0},{24,8},{1,17},{9,25},{17,1},{25,9},{2,18},{10... | collective-permute-start | bytes 786440 | tf_op jit(solution)/shard_map/ppermute | solution.py:19
  49.1 21.8 %copy-start.2 = (f32[512]{0:T(512)S(1)}, f32[512]{0:T(512)}, u32[]{:S(2)}) copy-start(f32[512]{0:T(512)} %param.293) | copy-start | bytes 6148
  49.1 21.9 %copy-start.4 = (s32[2]{0:T(128)S(1)}, s32[2]{0:T(128)}, u32[]{:S(2)}) copy-start(s32[2]{0:T(128)} %get-tuple-element.584.flags_ref) | copy-start | bytes 28
  49.1 10.8 %collective-permute-start.286 = (bf16[128,1024]{1,0:T(8,128)(2,1)S(1)}, bf16[128,1024]{1,0:T(8,128)(2,1)S(1)}, u32[]{:S(2)}, u32[]{:S(2)}) collective-permute-start(bf16[128,1024]{1,0:T(8,128)(2,1)S(1)} %get-tuple-element.603), channel_id=1, source_target_pairs={{0,8},{8,0},{16,24},{24,16},{1,9},{9,1},{17,25},{25,17},{2,10},{10... | collective-permute-start | bytes 786440 | tf_op jit(solution)/shard_map/ppermute | solution.py:19
  59.9 10.8 %all-to-all-start = ((f32[32,1,640]{2,1,0:T(1,128)}), f32[32,1,640]{2,1,0:T(1,128)S(1)}, u32[]{:S(2)}, u32[]{:S(2)}) async-start(f32[32,1,640]{2,1,0:T(1,128)} %get-tuple-element.597), calls=%async_computation | async-start | bytes 163840 | tf_op jit(solution)/shard_map/all_to_all | solution.py:27
  63.2 7.7 %collective-permute-start.289 = (bf16[4,128,1024]{2,1,0:T(8,128)(2,1)S(1)}, bf16[4,128,1024]{2,1,0:T(8,128)(2,1)S(1)}, u32[]{:S(2)}, u32[]{:S(2)}) collective-permute-start(bf16[4,128,1024]{2,1,0:T(8,128)(2,1)S(1)} %join.1.mine_ref), channel_id=1, source_target_pairs={{0,1},{1,0},{2,3},{3,2},{4,5},{5,4},{6,7},{7,6},{8,9},{9,8},{10,11... | collective-permute-start | bytes 3145736 | tf_op jit(solution)/shard_map/ppermute | solution.py:19
  70.9 1.6 %copy-start = (f32[512,1024]{1,0:T(8,128)S(1)}, f32[512,1024]{1,0:T(8,128)}, u32[]{:S(2)}) copy-start(f32[512,1024]{1,0:T(8,128)} %get-tuple-element.596.scores_ref) | copy-start | bytes 6291460
  75.5 1.1 %copy-start.5 = (bf16[512,1024]{1,0:T(8,128)(2,1)}, bf16[512,1024]{1,0:T(8,128)(2,1)S(1)}, u32[]{:S(2)}) copy-start(bf16[512,1024]{1,0:T(8,128)(2,1)S(1)} %get-tuple-element.598.grad_ref) | copy-start | bytes 3145732
  76.6 10.0 %all-to-all-start.1 = ((f32[32,1,512]{2,1,0:T(1,128)}), f32[32,1,512]{2,1,0:T(1,128)S(1)}, u32[]{:S(2)}, u32[]{:S(2)}) async-start(f32[32,1,512]{2,1,0:T(1,128)} %get-tuple-element.600), calls=%async_computation.1 | async-start | bytes 131072 | tf_op jit(solution)/shard_map/all_to_all | solution.py:27
where the time goes:
time: 87.3 us; the launch traced here: 87.2 us
  waiting for transfers between devices  34.1 us (39%)
  Pallas kernels  22.9 us (26%)
  starting transfers between devices  21.6 us (25%)
  local copies, waits for them, and re-layouts  6.33 us (7%)
  between operations  1.45 us (2%)
    ppermute x1, waiting for transfers between devices, over_chips(): return lax.ppermute(x, 'vocab', pairs)  26.9 us
    pallas_call x1, Pallas kernels, student_call(): pl.pallas_call(functools.partial(student_kernel, len(chunks)), in_specs=[...  10.2 us
    ppermute x8, starting transfers between devices, xor_permute(): return lax.ppermute(x, axis, [(i, i ^ k) for i in range(size)])  8.53 us
    pallas_call x1, Pallas kernels, head_grad_call(): pl.pallas_call(head_grad_kernel, grid=(rows // block,), in_specs=[pl.Bloc...  7.45 us
    ppermute x1, starting transfers between devices, over_chips(): return lax.ppermute(x, 'vocab', pairs)  7.33 us
    all_to_all x2, waiting for transfers between devices, exchange(): lax.all_to_all(copies, ('dp', 'vocab'), split_axis=0, concat_axis=0, tile...  7.18 us
    all_to_all x2, starting transfers between devices, exchange(): lax.all_to_all(copies, ('dp', 'vocab'), split_axis=0, concat_axis=0, tile...  5.71 us
    unnamed x16, local copies, waits for them, and re-layouts  4.51 us
  transfers between devices with their start and end apart: 11, of which 2 were waited for; matrix products, arithmetic and copies ran while one was open for 0% of the time, Pallas kernels for 23%

commit v1 on v0

--- a/solution.py
+++ b/solution.py
@@ -87,28 +87,32 @@
         copy.wait()
     hid_copy.start()
 
+    def scores_of(i):
+        columns = pl.ds(pl.multiple_of(i * block, block), block)
+        scores_ref[:, columns] = lax.dot_general(
+            hid_ref[...], rows_ref[columns], (((1,), (1,)), ((), ())), preferred_element_type=jnp.float32
+        )
+
+    def stats_of(i):
+        values = scores_ref[:, pl.ds(pl.multiple_of(i * block, block), block)]
+        old = top_ref[...]
+        top = jnp.maximum(old, jnp.max(values, axis=1, keepdims=True))
+        total = jnp.sum(jnp.exp(values - top), axis=1, keepdims=True)
+        top_ref[...] = top
+        sum_ref[...] = sum_ref[...] * jnp.exp(old - top) + total
+
     def step(i, carry):
-        columns = pl.ds(pl.multiple_of(i * block, block), block)
         head_copy(i).wait()
-        part = min(256, tokens)
-        for first in range(0, tokens, part):
-            here = slice(first, first + part)
-            scores = lax.dot_general(
-                hid_ref[here],
-                rows_ref[columns],
-                (((1,), (1,)), ((), ())),
-                preferred_element_type=jnp.float32,
-            )
-            scores_ref[here, columns] = scores
-            old = top_ref[here]
-            top = jnp.maximum(old, jnp.max(scores, axis=1, keepdims=True))
-            total = jnp.sum(jnp.exp(scores - top), axis=1, keepdims=True)
-            top_ref[here] = top
-            sum_ref[here] = sum_ref[here] * jnp.exp(old - top) + total
-        out_copy(i).start()
+        stats_of(i - 1)
+        scores_of(i)
+        out_copy(i - 1).start()
         return carry
 
-    lax.fori_loop(0, blocks, step, 0)
+    head_copy(0).wait()
+    scores_of(0)
+    lax.fori_loop(1, blocks, step, 0)
+    out_copy(blocks - 1).start()
+    stats_of(blocks - 1)
     at = place(own)
     for k in range(n_chunks):
         here = slice(k * own, (k + 1) * own)
@@ -158,67 +162,91 @@
 
 
 def logit_grad_kernel(
-    flags_ref, mine_ref, got_ref, scores_ref, row_s_ref, row_t_ref, weight_ref, grad_ref, cross_ref, col_ref
+    flags_ref, mine_ref, got_ref, scores_in_ref, row_s_ref, row_t_ref, weight_ref, out_ref, cross_ref,
+    target_ref, scores_ref, grad_ref, col_ref, target_sems, scores_sems, out_sems,
 ):
-    step, last = pl.program_id(0), pl.num_programs(0) - 1
-    rows = scores_ref.shape[0]
-    tokens = col_ref.shape[0]
+    n_dp, rows, _ = target_ref.shape
+    tokens = n_dp * rows
     half = rows // 2
-    at = place(rows)(step)
-
-    @pl.when(step == 0)
-    def _():
-        line = lax.broadcasted_iota(jnp.int32, (128, tokens), 0)
-        col_ref[...] = jnp.transpose(
-            jnp.where(line == 0, row_s_ref[...], jnp.where(line == 1, row_t_ref[...], weight_ref[...]))
+    at = place(rows)
+
+    def piece(k):
+        return pl.ds(pl.multiple_of(k * rows, rows), rows)
+
+    def target_copy(ref, k):
+        return pltpu.make_async_copy(ref.at[k], target_ref.at[k], target_sems.at[k])
+
+    def scores_copy(k):
+        return pltpu.make_async_copy(
+            scores_in_ref.at[piece(k)], scores_ref.at[piece(k)], scores_sems.at[k]
         )
 
-    keep = flags_ref[1] != 0
-    for first in (0, half):
-        part = slice(first, first + half)
-        here = pl.ds(pl.multiple_of(at + first, half), half)
-        cols = col_ref[here]
-        student = scores_ref[part]
-        target = jnp.where(keep, mine_ref[0, part], got_ref[0, part]).astype(jnp.float32)
-        prob_s = jnp.exp(student - cols[:, 0:1])
-        prob_t = jnp.exp(target - cols[:, 1:2])
-        cross = jnp.sum(prob_t * (target - student), axis=1, keepdims=True)
-        grad_ref[part] = (cols[:, 2:3] * (prob_s - prob_t)).astype(jnp.bfloat16)
-        col_ref[here] = jnp.broadcast_to(cross, (half, 128))
-
-    @pl.when(step == last)
-    def _():
-        cross = jnp.transpose(col_ref[...])[0:1]
-        cross_ref[...] = jnp.broadcast_to(cross[None], cross_ref.shape)
+    def out_copy(k):
+        return pltpu.make_async_copy(grad_ref.at[piece(k)], out_ref.at[piece(k)], out_sems.at[k])
+
+    for k in range(n_dp):
+        scores_copy(k).start()
+
+        @pl.when(flags_ref[1] != 0)
+        def _():
+            target_copy(mine_ref, k).start()
+
+        @pl.when(flags_ref[1] == 0)
+        def _():
+            target_copy(got_ref, k).start()
+
+    line = lax.broadcasted_iota(jnp.int32, (128, tokens), 0)
+    col_ref[...] = jnp.transpose(
+        jnp.where(line == 0, row_s_ref[...], jnp.where(line == 1, row_t_ref[...], weight_ref[...]))
+    )
+
+    def step(k, carry):
+        scores_copy(k).wait()
+        target_copy(mine_ref, k).wait()
+        for first in (0, half):
+            here = pl.ds(pl.multiple_of(at(k) + first, half), half)
+            part = pl.ds(pl.multiple_of(k * rows + first, half), half)
+            cols = col_ref[here]
+            student = scores_ref[part]
+            target = target_ref[k, first : first + half].astype(jnp.float32)
+            prob_s = jnp.exp(student - cols[:, 0:1])
+            prob_t = jnp.exp(target - cols[:, 1:2])
+            cross = jnp.sum(prob_t * (target - student), axis=1, keepdims=True)
+            grad_ref[part] = (cols[:, 2:3] * (prob_s - prob_t)).astype(jnp.bfloat16)
+            col_ref[here] = jnp.broadcast_to(cross, (half, 128))
+        out_copy(k).start()
+        return carry
+
+    lax.fori_loop(0, n_dp, step, 0)
+    cross = jnp.transpose(col_ref[...])[0:1]
+    cross_ref[...] = jnp.broadcast_to(cross[None], cross_ref.shape)
+    for k in range(n_dp):
+        out_copy(k).wait()
 
 
 def logit_grad_call(flags, mine, got, scores, total_s, total_t, weight):
     n_dp, part, rows = mine.shape
     tokens = n_dp * part
-    cross = (device_count(), 1, tokens)
-    whole_row = pl.BlockSpec((1, tokens), lambda k: (0, 0))
+    in_hbm = pl.BlockSpec(memory_space=pltpu.HBM)
+    in_vmem = pl.BlockSpec(memory_space=pltpu.VMEM)
     return pl.pallas_call(
         logit_grad_kernel,
-        grid=(n_dp,),
-        in_specs=[
-            pl.BlockSpec(memory_space=pltpu.SMEM),
-            pl.BlockSpec((1, part, rows), lambda k: (k, 0, 0)),
-            pl.BlockSpec((1, part, rows), lambda k: (k, 0, 0)),
-            pl.BlockSpec((part, rows), lambda k: (k, 0)),
-            whole_row,
-            whole_row,
-            whole_row,
-        ],
-        out_specs=[
-            pl.BlockSpec((part, rows), lambda k: (k, 0)),
-            pl.BlockSpec(cross, lambda k: (0, 0, 0)),
-        ],
+        in_specs=[pl.BlockSpec(memory_space=pltpu.SMEM)] + [in_hbm] * 3 + [in_vmem] * 3,
+        out_specs=[in_hbm, in_vmem],
         out_shape=[
             jax.ShapeDtypeStruct((tokens, rows), jnp.bfloat16),
-            jax.ShapeDtypeStruct(cross, jnp.float32),
+            jax.ShapeDtypeStruct((device_count(), 1, tokens), jnp.float32),
         ],
-        scratch_shapes=[pltpu.VMEM((tokens, 128), jnp.float32)],
-        compiler_params=pltpu.CompilerParams(vmem_limit_bytes=24 * MIB),
+        scratch_shapes=[
+            pltpu.VMEM(mine.shape, jnp.bfloat16),
+            pltpu.VMEM((tokens, rows), jnp.float32),
+            pltpu.VMEM((tokens, rows), jnp.bfloat16),
+            pltpu.VMEM((tokens, 128), jnp.float32),
+            pltpu.SemaphoreType.DMA((n_dp,)),
+            pltpu.SemaphoreType.DMA((n_dp,)),
+            pltpu.SemaphoreType.DMA((n_dp,)),
+        ],
+        compiler_params=pltpu.CompilerParams(vmem_limit_bytes=60 * MIB),
         cost_estimate=pl.CostEstimate(
             flops=8 * tokens * rows, bytes_accessed=8 * tokens * rows, transcendentals=2 * tokens * rows
         ),
@@ -226,25 +254,30 @@
     )(flags, mine, got, scores, total_s[None], total_t[None], weight[None])
 
 
-def head_grad_kernel(grad_ref, hid_ref, out_ref):
-    out_ref[0] = lax.dot_general(
-        grad_ref[...], hid_ref[...], (((0,), (0,)), ((), ())), preferred_element_type=jnp.float32
+def head_grad_kernel(grad_ref, hid_ref, out_ref, turned_ref):
+    @pl.when(pl.program_id(0) == 0)
+    def _():
+        turned_ref[...] = jnp.transpose(grad_ref[...])
+
+    out_ref[0] = jnp.dot(
+        turned_ref[...], hid_ref[...], preferred_element_type=jnp.float32
     ).astype(jnp.bfloat16)
 
 
 def head_grad_call(logit_grad, hid):
     tokens, rows = logit_grad.shape
     depth = hid.shape[1]
-    block = min(256, rows)
+    block = 512
     return pl.pallas_call(
         head_grad_kernel,
-        grid=(rows // block,),
+        grid=(depth // block,),
         in_specs=[
+            pl.BlockSpec((tokens, rows), lambda i: (0, 0)),
             pl.BlockSpec((tokens, block), lambda i: (0, i)),
-            pl.BlockSpec((tokens, depth), lambda i: (0, 0)),
         ],
-        out_specs=pl.BlockSpec((1, block, depth), lambda i: (0, i, 0)),
+        out_specs=pl.BlockSpec((1, rows, block), lambda i: (0, 0, i)),
         out_shape=jax.ShapeDtypeStruct((1, rows, depth), jnp.bfloat16),
+        scratch_shapes=[pltpu.VMEM((rows, tokens), jnp.bfloat16)],
         compiler_params=pltpu.CompilerParams(vmem_limit_bytes=60 * MIB),
         cost_estimate=pl.CostEstimate(
             flops=2 * tokens * rows * depth,

time: 87.3 us -> 101 us (1.16)
  starting transfers between devices: 21.6 us -> 31.2 us
  Pallas kernels: 22.9 us -> 25.4 us
  local copies, waits for them, and re-layouts: 6.33 us -> 4.4 us
  waiting for transfers between devices: 34.1 us -> 35.6 us
  other arithmetic: 0.84 us -> 2.01 us
    all_to_all x2, starting transfers between devices: 5.71 us -> 15.3 us  [exchange(): lax.all_to_all(copies, ('dp', 'vocab'), split_axis=0, concat_axis=0, tile...]
    pallas_call x2, Pallas kernels: 10.4 us -> 13.4 us  [the longest x1 8.47 us: head_grad_call(): pl.pallas_call(head_grad_kernel, grid=(depth // block,), in_specs=[pl.Blo...]
    unnamed x16 -> x14, local copies, waits for them, and re-layouts: 4.51 us -> 2.84 us
    add x2, other arithmetic: 0.01 us -> 1.19 us  [log_sum_exp(): return jnp.squeeze(top + jnp.log(total), axis)]
    ppermute x8, waiting for transfers between devices: 0.02 us -> 1.04 us  [xor_permute(): return lax.ppermute(x, axis, [(i, i ^ k) for i in range(size)])]
  transfers between devices with their start and end apart: 11 -> 11, of which waited for: 2 -> 4; matrix products, arithmetic and copies ran while one was open for 0% -> 1% of each run, Pallas kernels for 23% -> 21%
where the time goes in v1:
time: 101 us; the launch traced here: 100 us
  waiting for transfers between devices  35.6 us (35%)
  starting transfers between devices  31.2 us (31%)
  Pallas kernels  25.4 us (25%)
  local copies, waits for them, and re-layouts  4.4 us (4%)
  other arithmetic  2.01 us (2%)
  between operations  1.44 us (1%)
    ppermute x1, waiting for transfers between devices, over_chips(): return lax.ppermute(x, 'vocab', pairs)  27.4 us
    all_to_all x2, starting transfers between devices, exchange(): lax.all_to_all(copies, ('dp', 'vocab'), split_axis=0, concat_axis=0, tile...  15.3 us
    pallas_call x1, Pallas kernels, student_call(): pl.pallas_call(functools.partial(student_kernel, len(chunks)), in_specs=[...  9.84 us
    ppermute x8, starting transfers between devices, xor_permute(): return lax.ppermute(x, axis, [(i, i ^ k) for i in range(size)])  8.53 us
    pallas_call x1, Pallas kernels, head_grad_call(): pl.pallas_call(head_grad_kernel, grid=(depth // block,), in_specs=[pl.Blo...  8.47 us
    ppermute x1, starting transfers between devices, over_chips(): return lax.ppermute(x, 'vocab', pairs)  7.33 us
    all_to_all x2, waiting for transfers between devices, exchange(): lax.all_to_all(copies, ('dp', 'vocab'), split_axis=0, concat_axis=0, tile...  7.17 us
    pallas_call x1, Pallas kernels, logit_grad_call(): pl.pallas_call(logit_grad_kernel, in_specs=[pl.BlockSpec(memory_space=plt...  4.89 us
  transfers between devices with their start and end apart: 11, of which 4 were waited for; matrix products, arithmetic and copies ran while one was open for 1% of the time, Pallas kernels for 21%

profile of v1, /device:TPU:0, one launch (start us, length us, event | category | flops | bytes accessed | tf_op | source)
XLA Modules:
  0.0 100.1 jit_solution(18429543457446255598)
XLA Ops:
  0.6 0.5 collective-permute-start.285
  1.1 2.6 %collective-permute-start.283 = (bf16[128,3072]{1,0:T(8,128)(2,1)}, bf16[128,3072]{1,0:T(8,128)(2,1)S(1)}, u32[]{:S(2)}, u32[]{:S(2)}) collective-permute-start(bf16[128,3072]{1,0:T(8,128)(2,1)} %refs_0_), channel_id=1, source_target_pairs={{0,16},{8,24},{16,0},{24,8},{1,17},{9,25},{17,1},{25,9},{2,18},{10... | collective-permute-start | bytes 2359304 | tf_op jit(solution)/shard_map/ppermute | solution.py:19
  3.7 1.5 %collective-permute-start.282 = (bf16[128,3072]{1,0:T(8,128)(2,1)}, bf16[128,3072]{1,0:T(8,128)(2,1)}, u32[]{:S(2)}, u32[]{:S(2)}) collective-permute-start(bf16[128,3072]{1,0:T(8,128)(2,1)} %refs_0_), channel_id=1, source_target_pairs={{0,8},{8,0},{16,24},{24,16},{1,9},{9,1},{17,25},{25,17},{2,10},{10... | collective-permute-start | bytes 2359304 | tf_op jit(solution)/shard_map/ppermute | solution.py:19
  5.2 0.1 collective-permute-start.284
  5.3 1.5 %plan.1 = (s32[1]{0:T(128)}, s32[2]{0:T(128)}) custom-call(s32[8]{0:T(128)} %order_ref.1, s32[8,128]{1,0:T(8,128)} %constant.14.clone.codes_ref, s32[8,128]{1,0:T(8,128)} %constant.15.clone.keys_ref), custom_call_target="tpu_custom_call" | custom-call | tf_op jit(solution)/shard_map/plan/pallas_call | solution.py:343
  7.4 0.0 collective-permute-done.285.other_ref
  7.5 0.0 copy-start.1
  7.5 1.2 %copy-done.1 = bf16[128,4096]{1,0:T(8,128)(2,1)S(1)} copy-done((bf16[128,4096]{1,0:T(8,128)(2,1)S(1)}, bf16[128,4096]{1,0:T(8,128)(2,1)}, u32[]{:S(2)}) %copy-start.1) | copy-done | bytes 1048600
  8.7 0.0 copy-start.2
  8.7 0.6 copy-done.2
  9.3 0.7 pick.1
  10.0 34.8 %conditional.1 = (bf16[4,128,1024]{2,1,0:T(8,128)(2,1)}) conditional(s32[]{:T(128)} %bitcast, bf16[4,128,1024]{2,1,0:T(8,128)(2,1)S(1)} %pick.1, bf16[4,128,1024]{2,1,0:T(8,128)(2,1)S(1)} %pick.1, bf16[4,128,1024]{2,1,0:T(8,128)(2,1)S(1)} %pick.1, bf16[4,128,1024]{2,1,0:T(8,128)(2,1)S(1)} %pick.1, ...), branch_computations={%region_0.0_spmd, %region_1.0_spmd, %region_2.0_spmd, %region_3.0_... | conditional | bytes 4194352 | solution.py:427
  10.0 7.3 %collective-permute-start.4 = (bf16[4,128,1024]{2,1,0:T(8,128)(2,1)S(1)}, bf16[4,128,1024]{2,1,0:T(8,128)(2,1)}, u32[]{:S(2)}, u32[]{:S(2)}) collective-permute-start(bf16[4,128,1024]{2,1,0:T(8,128)(2,1)S(1)} %param.4), channel_id=1, source_target_pairs={{0,4},{1,7},{2,6},{3,3},{4,2},{5,5},{6,0},{7,1},{8,12},{9,15},{10,... | collective-permute-start | bytes 3145736 | tf_op jit(solution)/shard_map/cond/branch_4_fun/ppermute | solution.py:425
  17.3 27.4 %collective-permute-done.4 = bf16[4,128,1024]{2,1,0:T(8,128)(2,1)} collective-permute-done((bf16[4,128,1024]{2,1,0:T(8,128)(2,1)S(1)}, bf16[4,128,1024]{2,1,0:T(8,128)(2,1)}, u32[]{:S(2)}, u32[]{:S(2)}) %collective-permute-start.4) | collective-permute-done | bytes 1048608 | tf_op jit(solution)/shard_map/cond/branch_4_fun/ppermute | solution.py:425
  44.7 0.0 collective-permute-done.283.refs_2_
  44.7 0.0 copy-start.6
  44.7 0.0 collective-permute-done.282.refs_1_
  44.7 0.0 collective-permute-done.284.refs_3_
  44.7 1.5 %slice_bitcast_fusion = (bf16[128,1024]{1,0:T(8,128)(2,1)S(1)}, bf16[128,1024]{1,0:T(8,128)(2,1)S(1)}, bf16[128,1024]{1,0:T(8,128)(2,1)S(1)}, bf16[128,1024]{1,0:T(8,128)(2,1)S(1)}) fusion(bf16[4,128,1024]{2,1,0:T(8,128)(2,1)} %get-tuple-element.607), kind=kLoop, calls=%fused_computation | loop fusion | bytes 2097152 | tf_op jit(solution)/shard_map/squeeze | solution.py:433
  46.3 2.5 %collective-permute-start.288 = (bf16[128,1024]{1,0:T(8,128)(2,1)S(1)}, bf16[128,1024]{1,0:T(8,128)(2,1)S(1)}, u32[]{:S(2)}, u32[]{:S(2)}) collective-permute-start(bf16[128,1024]{1,0:T(8,128)(2,1)S(1)} %get-tuple-element.601), channel_id=1, source_target_pairs={{0,24},{8,16},{16,8},{24,0},{1,25},{9,17},{17,9},{25,1},{2,26},{10... | collective-permute-start | bytes 786440 | tf_op jit(solution)/shard_map/ppermute | solution.py:19
  48.8 0.5 collective-permute-start.287
  49.3 0.5 collective-permute-start.286
  49.9 0.0 copy-done.6
  49.9 9.8 %student.1 = (f32[512,1024]{1,0:T(8,128)}, bf16[512,3072]{1,0:T(8,128)(2,1)}, f32[32,1,640]{2,1,0:T(1,128)}) custom-call(bf16[128,3072]{1,0:T(8,128)(2,1)} %refs_0_, bf16[128,3072]{1,0:T(8,128)(2,1)} %collective-permute-done.282.refs_1_, bf16[128,3072]{1,0:T(8,128)(2,1)} %copy-done.6, bf16[128,3072]{1,0:T(8,128)(2,1)} %collective-permute-done.284.refs_3_, ...), custom_call_target="tpu_custom_call" | custom-call | flops 3221225472 | bytes 11534336 | tf_op jit(solution)/shard_map/student/pallas_call | solution.py:132
  59.7 0.0 collective-permute-done.288.refs_3_
  59.7 0.9 collective-permute-done.287.refs_2_
  60.7 0.1 collective-permute-done.286.refs_1_
  60.8 12.8 %all-to-all-start = ((f32[32,1,640]{2,1,0:T(1,128)}), f32[32,1,640]{2,1,0:T(1,128)S(1)}, u32[]{:S(2)}, u32[]{:S(2)}) async-start(f32[32,1,640]{2,1,0:T(1,128)} %get-tuple-element.597), calls=%async_computation | async-start | bytes 163840 | tf_op jit(solution)/shard_map/all_to_all | solution.py:27
  73.6 0.1 join.1.mine_ref
  73.6 0.0 copy-start
  73.6 0.3 collective-permute-start.289
  74.0 7.2 %all-to-all-done = f32[32,1,640]{2,1,0:T(1,128)S(1)} async-done(((f32[32,1,640]{2,1,0:T(1,128)}), f32[32,1,640]{2,1,0:T(1,128)S(1)}, u32[]{:S(2)}, u32[]{:S(2)}) %all-to-all-start) | async-done | bytes 81952 | tf_op jit(solution)/shard_map/all_to_all | solution.py:27
  81.2 0.1 fusion.5
  81.3 0.6 log_add_fusion.1
  81.9 0.6 log_add_fusion
  82.5 0.0 collective-permute-done.289.got_ref
  82.5 0.0 copy-done
  82.5 1.0 copy-done.3
  83.5 4.9 %logit_grad.1 = (bf16[512,1024]{1,0:T(8,128)(2,1)}, f32[32,1,512]{2,1,0:T(1,128)}) custom-call(s32[2]{0:T(128)} %get-tuple-element.584.flags_ref, bf16[4,128,1024]{2,1,0:T(8,128)(2,1)} %copy-done, bf16[4,128,1024]{2,1,0:T(8,128)(2,1)} %copy-done.3, f32[512,1024]{1,0:T(8,128)} %get-tuple-element.596.scores_in_ref, f32[1,512]{1,0:T(1,128)} %bitcast.33, ...), custom_call_target="tpu_custom_call" | custom-call | flops 4194304 | bytes 4194304 | tf_op jit(solution)/shard_map/logit_grad/pallas_call | solution.py:232
  88.4 0.0 copy-start.4
  88.4 0.0 copy-start.5
  88.4 2.5 %all-to-all-start.1 = ((f32[32,1,512]{2,1,0:T(1,128)}), f32[32,1,512]{2,1,0:T(1,128)S(1)}, u32[]{:S(2)}, u32[]{:S(2)}) async-start(f32[32,1,512]{2,1,0:T(1,128)} %get-tuple-element.600), calls=%async_computation.1 | async-start | bytes 131072 | tf_op jit(solution)/shard_map/all_to_all | solution.py:27
  91.0 8.5 %head_grad.1 = bf16[1,1024,3072]{2,1,0:T(8,128)(2,1)} custom-call(bf16[512,1024]{1,0:T(8,128)(2,1)} %get-tuple-element.598.grad_ref, bf16[512,3072]{1,0:T(8,128)(2,1)} %get-tuple-element.599.hid_ref), custom_call_target="tpu_custom_call" | custom-call | flops 3221225472 | bytes 9437184 | tf_op jit(solution)/shard_map/head_grad/pallas_call | solution.py:271
  99.4 0.0 all-to-all-done.1
  99.4 0.1 reduce_sum.29
  99.5 0.0 copy-done.4
  99.5 0.0 copy-done.5
  99.5 0.6 fusion.4
  (5 shorter events, 0.1 us)
Async XLA Ops:
  0.6 6.8 %collective-permute-start.285 = (bf16[128,4096]{1,0:T(8,128)(2,1)}, bf16[128,4096]{1,0:T(8,128)(2,1)S(1)}, u32[]{:S(2)}, u32[]{:S(2)}) collective-permute-start(bf16[128,4096]{1,0:T(8,128)(2,1)} %refs_5_.1), channel_id=1, source_target_pairs={{0,1},{1,0},{2,3},{3,2},{4,5},{5,4},{6,7},{7,6},{8,9},{9,8},{10,11... | collective-permute-start | bytes 3145736 | tf_op jit(solution)/shard_map/ppermute | solution.py:19
  1.1 43.6 %collective-permute-start.283 = (bf16[128,3072]{1,0:T(8,128)(2,1)}, bf16[128,3072]{1,0:T(8,128)(2,1)S(1)}, u32[]{:S(2)}, u32[]{:S(2)}) collective-permute-start(bf16[128,3072]{1,0:T(8,128)(2,1)} %refs_0_), channel_id=1, source_target_pairs={{0,16},{8,24},{16,0},{24,8},{1,17},{9,25},{17,1},{25,9},{2,18},{10... | collective-permute-start | bytes 2359304 | tf_op jit(solution)/shard_map/ppermute | solution.py:19
  3.7 41.0 %collective-permute-start.282 = (bf16[128,3072]{1,0:T(8,128)(2,1)}, bf16[128,3072]{1,0:T(8,128)(2,1)}, u32[]{:S(2)}, u32[]{:S(2)}) collective-permute-start(bf16[128,3072]{1,0:T(8,128)(2,1)} %refs_0_), channel_id=1, source_target_pairs={{0,8},{8,0},{16,24},{24,16},{1,9},{9,1},{17,25},{25,17},{2,10},{10... | collective-permute-start | bytes 2359304 | tf_op jit(solution)/shard_map/ppermute | solution.py:19
  5.2 39.5 %collective-permute-start.284 = (bf16[128,3072]{1,0:T(8,128)(2,1)}, bf16[128,3072]{1,0:T(8,128)(2,1)}, u32[]{:S(2)}, u32[]{:S(2)}) collective-permute-start(bf16[128,3072]{1,0:T(8,128)(2,1)} %refs_0_), channel_id=1, source_target_pairs={{0,24},{8,16},{16,8},{24,0},{1,25},{9,17},{17,9},{25,1},{2,26},{10... | collective-permute-start | bytes 2359304 | tf_op jit(solution)/shard_map/ppermute | solution.py:19
  7.5 1.2 %copy-start.1 = (bf16[128,4096]{1,0:T(8,128)(2,1)S(1)}, bf16[128,4096]{1,0:T(8,128)(2,1)}, u32[]{:S(2)}) copy-start(bf16[128,4096]{1,0:T(8,128)(2,1)} %refs_5_.1) | copy-start | bytes 3145732
  8.7 0.6 copy-start.2
  10.0 34.7 %collective-permute-start.4 = (bf16[4,128,1024]{2,1,0:T(8,128)(2,1)S(1)}, bf16[4,128,1024]{2,1,0:T(8,128)(2,1)}, u32[]{:S(2)}, u32[]{:S(2)}) collective-permute-start(bf16[4,128,1024]{2,1,0:T(8,128)(2,1)S(1)} %param.4), channel_id=1, source_target_pairs={{0,4},{1,7},{2,6},{3,3},{4,2},{5,5},{6,0},{7,1},{8,12},{9,15},{10,... | collective-permute-start | bytes 3145736 | tf_op jit(solution)/shard_map/cond/branch_4_fun/ppermute | solution.py:425
  44.7 5.1 %copy-start.6 = (bf16[128,3072]{1,0:T(8,128)(2,1)}, bf16[128,3072]{1,0:T(8,128)(2,1)S(1)}, u32[]{:S(2)}) copy-start(bf16[128,3072]{1,0:T(8,128)(2,1)S(1)} %collective-permute-done.283.refs_2_) | copy-start | bytes 2359300
  46.3 13.4 %collective-permute-start.288 = (bf16[128,1024]{1,0:T(8,128)(2,1)S(1)}, bf16[128,1024]{1,0:T(8,128)(2,1)S(1)}, u32[]{:S(2)}, u32[]{:S(2)}) collective-permute-start(bf16[128,1024]{1,0:T(8,128)(2,1)S(1)} %get-tuple-element.601), channel_id=1, source_target_pairs={{0,24},{8,16},{16,8},{24,0},{1,25},{9,17},{17,9},{25,1},{2,26},{10... | collective-permute-start | bytes 786440 | tf_op jit(solution)/shard_map/ppermute | solution.py:19
  48.8 11.9 %collective-permute-start.287 = (bf16[128,1024]{1,0:T(8,128)(2,1)S(1)}, bf16[128,1024]{1,0:T(8,128)(2,1)S(1)}, u32[]{:S(2)}, u32[]{:S(2)}) collective-permute-start(bf16[128,1024]{1,0:T(8,128)(2,1)S(1)} %get-tuple-element.602), channel_id=1, source_target_pairs={{0,16},{8,24},{16,0},{24,8},{1,17},{9,25},{17,1},{25,9},{2,18},{10... | collective-permute-start | bytes 786440 | tf_op jit(solution)/shard_map/ppermute | solution.py:19
  49.3 11.4 %collective-permute-start.286 = (bf16[128,1024]{1,0:T(8,128)(2,1)S(1)}, bf16[128,1024]{1,0:T(8,128)(2,1)S(1)}, u32[]{:S(2)}, u32[]{:S(2)}) collective-permute-start(bf16[128,1024]{1,0:T(8,128)(2,1)S(1)} %get-tuple-element.603), channel_id=1, source_target_pairs={{0,8},{8,0},{16,24},{24,16},{1,9},{9,1},{17,25},{25,17},{2,10},{10... | collective-permute-start | bytes 786440 | tf_op jit(solution)/shard_map/ppermute | solution.py:19
  60.8 20.4 %all-to-all-start = ((f32[32,1,640]{2,1,0:T(1,128)}), f32[32,1,640]{2,1,0:T(1,128)S(1)}, u32[]{:S(2)}, u32[]{:S(2)}) async-start(f32[32,1,640]{2,1,0:T(1,128)} %get-tuple-element.597), calls=%async_computation | async-start | bytes 163840 | tf_op jit(solution)/shard_map/all_to_all | solution.py:27
  73.6 8.9 %copy-start = (bf16[4,128,1024]{2,1,0:T(8,128)(2,1)}, bf16[4,128,1024]{2,1,0:T(8,128)(2,1)S(1)}, u32[]{:S(2)}) copy-start(bf16[4,128,1024]{2,1,0:T(8,128)(2,1)S(1)} %join.1.mine_ref) | copy-start | bytes 3145732
  73.6 8.9 %collective-permute-start.289 = (bf16[4,128,1024]{2,1,0:T(8,128)(2,1)S(1)}, bf16[4,128,1024]{2,1,0:T(8,128)(2,1)S(1)}, u32[]{:S(2)}, u32[]{:S(2)}) collective-permute-start(bf16[4,128,1024]{2,1,0:T(8,128)(2,1)S(1)} %join.1.mine_ref), channel_id=1, source_target_pairs={{0,1},{1,0},{2,3},{3,2},{4,5},{5,4},{6,7},{7,6},{8,9},{9,8},{10,11... | collective-permute-start | bytes 3145736 | tf_op jit(solution)/shard_map/ppermute | solution.py:19
  82.5 1.0 copy-start.3
  88.4 11.1 %copy-start.4 = (f32[512]{0:T(512)S(1)}, f32[512]{0:T(512)}, u32[]{:S(2)}) copy-start(f32[512]{0:T(512)} %log_add_fusion.1) | copy-start | bytes 6148
  88.4 11.1 %copy-start.5 = (f32[4,128]{1,0:T(4,128)S(1)}, f32[4,128]{1,0:T(4,128)}, u32[]{:S(2)}) copy-start(f32[4,128]{1,0:T(4,128)} %log_add_fusion) | copy-start | bytes 6148
  88.4 11.0 %all-to-all-start.1 = ((f32[32,1,512]{2,1,0:T(1,128)}), f32[32,1,512]{2,1,0:T(1,128)S(1)}, u32[]{:S(2)}, u32[]{:S(2)}) async-start(f32[32,1,512]{2,1,0:T(1,128)} %get-tuple-element.600), calls=%async_computation.1 | async-start | bytes 131072 | tf_op jit(solution)/shard_map/all_to_all | solution.py:27

commit v2 on v0

--- a/solution.py
+++ b/solution.py
@@ -87,28 +87,32 @@
         copy.wait()
     hid_copy.start()
 
+    def scores_of(i):
+        columns = pl.ds(pl.multiple_of(i * block, block), block)
+        scores_ref[:, columns] = lax.dot_general(
+            hid_ref[...], rows_ref[columns], (((1,), (1,)), ((), ())), preferred_element_type=jnp.float32
+        )
+
+    def stats_of(i):
+        values = scores_ref[:, pl.ds(pl.multiple_of(i * block, block), block)]
+        old = top_ref[...]
+        top = jnp.maximum(old, jnp.max(values, axis=1, keepdims=True))
+        total = jnp.sum(jnp.exp(values - top), axis=1, keepdims=True)
+        top_ref[...] = top
+        sum_ref[...] = sum_ref[...] * jnp.exp(old - top) + total
+
     def step(i, carry):
-        columns = pl.ds(pl.multiple_of(i * block, block), block)
         head_copy(i).wait()
-        part = min(256, tokens)
-        for first in range(0, tokens, part):
-            here = slice(first, first + part)
-            scores = lax.dot_general(
-                hid_ref[here],
-                rows_ref[columns],
-                (((1,), (1,)), ((), ())),
-                preferred_element_type=jnp.float32,
-            )
-            scores_ref[here, columns] = scores
-            old = top_ref[here]
-            top = jnp.maximum(old, jnp.max(scores, axis=1, keepdims=True))
-            total = jnp.sum(jnp.exp(scores - top), axis=1, keepdims=True)
-            top_ref[here] = top
-            sum_ref[here] = sum_ref[here] * jnp.exp(old - top) + total
-        out_copy(i).start()
+        stats_of(i - 1)
+        scores_of(i)
+        out_copy(i - 1).start()
         return carry
 
-    lax.fori_loop(0, blocks, step, 0)
+    head_copy(0).wait()
+    scores_of(0)
+    lax.fori_loop(1, blocks, step, 0)
+    out_copy(blocks - 1).start()
+    stats_of(blocks - 1)
     at = place(own)
     for k in range(n_chunks):
         here = slice(k * own, (k + 1) * own)
@@ -157,10 +161,62 @@
     )(*chunks, head, teacher)
 
 
+def cross_kernel(flags_ref, mine_ref, got_ref, scores_ref, out_ref, col_ref):
+    step, last = pl.program_id(0), pl.num_programs(0) - 1
+    rows = scores_ref.shape[0]
+    tokens = col_ref.shape[0]
+    half = rows // 2
+    at = place(rows)(step)
+    keep = flags_ref[1] != 0
+    lane = lax.broadcasted_iota(jnp.int32, (half, 128), 1)
+    for first in (0, half):
+        part = slice(first, first + half)
+        here = pl.ds(pl.multiple_of(at + first, half), half)
+        target = jnp.where(keep, mine_ref[0, part], got_ref[0, part]).astype(jnp.float32)
+        top = jnp.max(target, axis=1, keepdims=True)
+        cross = jnp.exp(target - top) * (target - scores_ref[part])
+        col_ref[here] = jnp.where(lane == 0, top, jnp.sum(cross, axis=1, keepdims=True))
+
+    @pl.when(step == last)
+    def _():
+        lines = jnp.transpose(col_ref[...])
+        for i in range(2):
+            line = jnp.broadcast_to(lines[i : i + 1][None], (out_ref.shape[0], 1, tokens))
+            out_ref[:, :, i * tokens : (i + 1) * tokens] = line
+
+
+def block_specs(n_dp, part, rows):
+    return [
+        pl.BlockSpec(memory_space=pltpu.SMEM),
+        pl.BlockSpec((1, part, rows), lambda k: (k, 0, 0)),
+        pl.BlockSpec((1, part, rows), lambda k: (k, 0, 0)),
+        pl.BlockSpec((part, rows), lambda k: (k, 0)),
+    ]
+
+
+def cross_call(flags, mine, got, scores):
+    n_dp, part, rows = mine.shape
+    tokens = n_dp * part
+    shape = (device_count(), 1, 2 * tokens)
+    return pl.pallas_call(
+        cross_kernel,
+        grid=(n_dp,),
+        in_specs=block_specs(n_dp, part, rows),
+        out_specs=pl.BlockSpec(shape, lambda k: (0, 0, 0)),
+        out_shape=jax.ShapeDtypeStruct(shape, jnp.float32),
+        scratch_shapes=[pltpu.VMEM((tokens, 128), jnp.float32)],
+        compiler_params=pltpu.CompilerParams(vmem_limit_bytes=24 * MIB),
+        cost_estimate=pl.CostEstimate(
+            flops=5 * tokens * rows, bytes_accessed=8 * tokens * rows, transcendentals=tokens * rows
+        ),
+        name="cross",
+    )(flags, mine, got, scores)
+
+
 def logit_grad_kernel(
-    flags_ref, mine_ref, got_ref, scores_ref, row_s_ref, row_t_ref, weight_ref, grad_ref, cross_ref, col_ref
+    flags_ref, mine_ref, got_ref, scores_ref, row_s_ref, row_t_ref, weight_ref, grad_ref, col_ref
 ):
-    step, last = pl.program_id(0), pl.num_programs(0) - 1
+    step = pl.program_id(0)
     rows = scores_ref.shape[0]
     tokens = col_ref.shape[0]
     half = rows // 2
@@ -176,51 +232,27 @@
     keep = flags_ref[1] != 0
     for first in (0, half):
         part = slice(first, first + half)
-        here = pl.ds(pl.multiple_of(at + first, half), half)
-        cols = col_ref[here]
-        student = scores_ref[part]
+        cols = col_ref[pl.ds(pl.multiple_of(at + first, half), half)]
         target = jnp.where(keep, mine_ref[0, part], got_ref[0, part]).astype(jnp.float32)
-        prob_s = jnp.exp(student - cols[:, 0:1])
+        prob_s = jnp.exp(scores_ref[part] - cols[:, 0:1])
         prob_t = jnp.exp(target - cols[:, 1:2])
-        cross = jnp.sum(prob_t * (target - student), axis=1, keepdims=True)
         grad_ref[part] = (cols[:, 2:3] * (prob_s - prob_t)).astype(jnp.bfloat16)
-        col_ref[here] = jnp.broadcast_to(cross, (half, 128))
-
-    @pl.when(step == last)
-    def _():
-        cross = jnp.transpose(col_ref[...])[0:1]
-        cross_ref[...] = jnp.broadcast_to(cross[None], cross_ref.shape)
 
 
 def logit_grad_call(flags, mine, got, scores, total_s, total_t, weight):
     n_dp, part, rows = mine.shape
     tokens = n_dp * part
-    cross = (device_count(), 1, tokens)
     whole_row = pl.BlockSpec((1, tokens), lambda k: (0, 0))
     return pl.pallas_call(
         logit_grad_kernel,
         grid=(n_dp,),
-        in_specs=[
-            pl.BlockSpec(memory_space=pltpu.SMEM),
-            pl.BlockSpec((1, part, rows), lambda k: (k, 0, 0)),
-            pl.BlockSpec((1, part, rows), lambda k: (k, 0, 0)),
-            pl.BlockSpec((part, rows), lambda k: (k, 0)),
-            whole_row,
-            whole_row,
-            whole_row,
-        ],
-        out_specs=[
-            pl.BlockSpec((part, rows), lambda k: (k, 0)),
-            pl.BlockSpec(cross, lambda k: (0, 0, 0)),
-        ],
-        out_shape=[
-            jax.ShapeDtypeStruct((tokens, rows), jnp.bfloat16),
-            jax.ShapeDtypeStruct(cross, jnp.float32),
-        ],
+        in_specs=block_specs(n_dp, part, rows) + [whole_row] * 3,
+        out_specs=pl.BlockSpec((part, rows), lambda k: (k, 0)),
+        out_shape=jax.ShapeDtypeStruct((tokens, rows), jnp.bfloat16),
         scratch_shapes=[pltpu.VMEM((tokens, 128), jnp.float32)],
         compiler_params=pltpu.CompilerParams(vmem_limit_bytes=24 * MIB),
         cost_estimate=pl.CostEstimate(
-            flops=8 * tokens * rows, bytes_accessed=8 * tokens * rows, transcendentals=2 * tokens * rows
+            flops=4 * tokens * rows, bytes_accessed=8 * tokens * rows, transcendentals=2 * tokens * rows
         ),
         name="logit_grad",
     )(flags, mine, got, scores, total_s[None], total_t[None], weight[None])
@@ -413,9 +445,11 @@
         flags, got = jnp.ones((2,), jnp.int32), mine
 
     total_s, total_t = combine_stats(exchange(stats), tokens)
-    logit_grad, cross = logit_grad_call(flags, mine, got, student, total_s, total_t, loss_weight)
+    parts = exchange(cross_call(flags, mine, got, student))
+    logit_grad = logit_grad_call(flags, mine, got, student, total_s, total_t, loss_weight)
     head_grad = head_grad_call(logit_grad, hid)
-    divergence = jnp.sum(exchange(cross), axis=(0, 1)) - total_t + total_s
+    tops, terms = parts[:, 0, :tokens], parts[:, 0, tokens:]
+    divergence = jnp.sum(terms * jnp.exp(tops - total_t), axis=0) - total_t + total_s
     return head_grad, divergence
 
 

time: 87.3 us -> 111 us (1.27)
  blocking collectives: 0 us -> 12.8 us
  starting transfers between devices: 21.6 us -> 27 us
  local copies, waits for them, and re-layouts: 6.33 us -> 10.4 us
  waiting for transfers between devices: 34.1 us -> 35.4 us
    all_to_all x0 -> x1, blocking collectives: none -> 12.8 us  [exchange(): lax.all_to_all(copies, ('dp', 'vocab'), split_axis=0, concat_axis=0, tile...]
    ppermute x8, starting transfers between devices: 8.53 us -> 17.1 us  [xor_permute(): return lax.ppermute(x, axis, [(i, i ^ k) for i in range(size)])]
    unnamed x16 -> x26, local copies, waits for them, and re-layouts: 4.51 us -> 8.52 us
    all_to_all x2 -> x1, starting transfers between devices: 5.71 us -> 2.56 us  [exchange(): lax.all_to_all(copies, ('dp', 'vocab'), split_axis=0, concat_axis=0, tile...]
    pallas_call x1 -> x2, Pallas kernels: 2.96 us -> 4.22 us  [the longest x1 2.45 us: cross_call(): pl.pallas_call(cross_kernel, grid=(n_dp,), in_specs=block_specs(n_dp, par...]
    all_to_all x2 -> x1, waiting for transfers between devices: 7.18 us -> 8.07 us  [exchange(): lax.all_to_all(copies, ('dp', 'vocab'), split_axis=0, concat_axis=0, tile...]
  transfers between devices with their start and end apart: 11 -> 10, of which waited for: 2 -> 2; matrix products, arithmetic and copies ran while one was open for 0% -> 0% of each run, Pallas kernels for 23% -> 11%
where the time goes in v2:
time: 111 us; the launch traced here: 112 us
  waiting for transfers between devices  35.4 us (32%)
  starting transfers between devices  27 us (24%)
  Pallas kernels  23.7 us (21%)
  blocking collectives  12.8 us (12%)
  local copies, waits for them, and re-layouts  10.4 us (9%)
  between operations  1.47 us (1%)
    ppermute x1, waiting for transfers between devices, over_chips(): return lax.ppermute(x, 'vocab', pairs)  27.3 us
    ppermute x8, starting transfers between devices, xor_permute(): return lax.ppermute(x, axis, [(i, i ^ k) for i in range(size)])  17.1 us
    all_to_all x1, blocking collectives, exchange(): lax.all_to_all(copies, ('dp', 'vocab'), split_axis=0, concat_axis=0, tile...  12.8 us
    pallas_call x1, Pallas kernels, student_call(): pl.pallas_call(functools.partial(student_kernel, len(chunks)), in_specs=[...  9.84 us
    unnamed x26, local copies, waits for them, and re-layouts  8.52 us
    all_to_all x1, waiting for transfers between devices, exchange(): lax.all_to_all(copies, ('dp', 'vocab'), split_axis=0, concat_axis=0, tile...  8.07 us
    pallas_call x1, Pallas kernels, head_grad_call(): pl.pallas_call(head_grad_kernel, grid=(rows // block,), in_specs=[pl.Bloc...  7.44 us
    ppermute x1, starting transfers between devices, over_chips(): return lax.ppermute(x, 'vocab', pairs)  7.33 us
  transfers between devices with their start and end apart: 10, of which 2 were waited for; matrix products, arithmetic and copies ran while one was open for 0% of the time, Pallas kernels for 11%

profile of v2, /device:TPU:0, one launch (start us, length us, event | category | flops | bytes accessed | tf_op | source)
XLA Modules:
  0.0 111.5 jit_solution(11415792633975372359)
XLA Ops:
  0.6 0.5 collective-permute-start.285
  1.1 2.6 %collective-permute-start.283 = (bf16[128,3072]{1,0:T(8,128)(2,1)}, bf16[128,3072]{1,0:T(8,128)(2,1)S(1)}, u32[]{:S(2)}, u32[]{:S(2)}) collective-permute-start(bf16[128,3072]{1,0:T(8,128)(2,1)} %refs_0_), channel_id=1, source_target_pairs={{0,16},{8,24},{16,0},{24,8},{1,17},{9,25},{17,1},{25,9},{2,18},{10... | collective-permute-start | bytes 2359304 | tf_op jit(solution)/shard_map/ppermute | solution.py:19
  3.7 1.5 %collective-permute-start.282 = (bf16[128,3072]{1,0:T(8,128)(2,1)}, bf16[128,3072]{1,0:T(8,128)(2,1)S(1)}, u32[]{:S(2)}, u32[]{:S(2)}) collective-permute-start(bf16[128,3072]{1,0:T(8,128)(2,1)} %refs_0_), channel_id=1, source_target_pairs={{0,8},{8,0},{16,24},{24,16},{1,9},{9,1},{17,25},{25,17},{2,10},{10... | collective-permute-start | bytes 2359304 | tf_op jit(solution)/shard_map/ppermute | solution.py:19
  5.2 0.1 collective-permute-start.284
  5.3 1.5 %plan.1 = (s32[1]{0:T(128)}, s32[2]{0:T(128)}) custom-call(s32[8]{0:T(128)} %order_ref.1, s32[8,128]{1,0:T(8,128)} %constant.14.clone.codes_ref, s32[8,128]{1,0:T(8,128)} %constant.15.clone.keys_ref), custom_call_target="tpu_custom_call" | custom-call | tf_op jit(solution)/shard_map/plan/pallas_call | solution.py:342
  7.4 0.0 collective-permute-done.285.other_ref
  7.5 0.0 copy-start.4
  7.5 1.2 %copy-done.4 = bf16[128,4096]{1,0:T(8,128)(2,1)S(1)} copy-done((bf16[128,4096]{1,0:T(8,128)(2,1)S(1)}, bf16[128,4096]{1,0:T(8,128)(2,1)}, u32[]{:S(2)}) %copy-start.4) | copy-done | bytes 1048600
  8.7 0.7 copy-done.8
  9.3 0.7 pick.1
  10.0 34.7 %conditional.1 = (bf16[4,128,1024]{2,1,0:T(8,128)(2,1)}) conditional(s32[]{:T(128)} %bitcast, bf16[4,128,1024]{2,1,0:T(8,128)(2,1)S(1)} %pick.1, bf16[4,128,1024]{2,1,0:T(8,128)(2,1)S(1)} %pick.1, bf16[4,128,1024]{2,1,0:T(8,128)(2,1)S(1)} %pick.1, bf16[4,128,1024]{2,1,0:T(8,128)(2,1)S(1)} %pick.1, ...), branch_computations={%region_0.0_spmd, %region_1.0_spmd, %region_2.0_spmd, %region_3.0_... | conditional | bytes 4194352 | solution.py:426
  10.1 7.3 %collective-permute-start.76 = (bf16[4,128,1024]{2,1,0:T(8,128)(2,1)S(1)}, bf16[4,128,1024]{2,1,0:T(8,128)(2,1)}, u32[]{:S(2)}, u32[]{:S(2)}) collective-permute-start(bf16[4,128,1024]{2,1,0:T(8,128)(2,1)S(1)} %param.76), channel_id=1, source_target_pairs={{0,4},{1,7},{2,6},{3,3},{4,2},{5,1},{6,0},{7,5},{8,12},{9,15},{10,... | collective-permute-start | bytes 3145736 | tf_op jit(solution)/shard_map/cond/branch_76_fun/ppermute | solution.py:424
  17.4 27.3 %collective-permute-done.76 = bf16[4,128,1024]{2,1,0:T(8,128)(2,1)} collective-permute-done((bf16[4,128,1024]{2,1,0:T(8,128)(2,1)S(1)}, bf16[4,128,1024]{2,1,0:T(8,128)(2,1)}, u32[]{:S(2)}, u32[]{:S(2)}) %collective-permute-start.76) | collective-permute-done | bytes 1048608 | tf_op jit(solution)/shard_map/cond/branch_76_fun/ppermute | solution.py:424
  44.7 0.0 collective-permute-done.283.refs_2_
  44.7 0.0 collective-permute-done.282.refs_1_
  44.7 0.0 copy-start.12
  44.7 0.0 collective-permute-done.284.refs_3_
  44.7 1.8 %slice_bitcast_fusion = (bf16[128,1024]{1,0:T(8,128)(2,1)S(1)}, bf16[128,1024]{1,0:T(8,128)(2,1)S(1)}, bf16[128,1024]{1,0:T(8,128)(2,1)S(1)}, bf16[128,1024]{1,0:T(8,128)(2,1)S(1)}) fusion(bf16[4,128,1024]{2,1,0:T(8,128)(2,1)} %get-tuple-element.609), kind=kLoop, calls=%fused_computation | loop fusion | bytes 2097152 | tf_op jit(solution)/shard_map/squeeze | solution.py:432
  46.5 2.5 %collective-permute-start.288 = (bf16[128,1024]{1,0:T(8,128)(2,1)S(1)}, bf16[128,1024]{1,0:T(8,128)(2,1)S(1)}, u32[]{:S(2)}, u32[]{:S(2)}) collective-permute-start(bf16[128,1024]{1,0:T(8,128)(2,1)S(1)} %get-tuple-element.599), channel_id=1, source_target_pairs={{0,24},{8,16},{16,8},{24,0},{1,25},{9,17},{17,9},{25,1},{2,26},{10... | collective-permute-start | bytes 786440 | tf_op jit(solution)/shard_map/ppermute | solution.py:19
  49.0 0.5 collective-permute-start.287
  49.5 0.5 collective-permute-start.286
  50.1 0.0 copy-done.11
  50.1 0.0 copy-done.12
  50.1 9.8 %student.1 = (f32[512,1024]{1,0:T(8,128)}, bf16[512,3072]{1,0:T(8,128)(2,1)}, f32[32,1,640]{2,1,0:T(1,128)}) custom-call(bf16[128,3072]{1,0:T(8,128)(2,1)} %refs_0_, bf16[128,3072]{1,0:T(8,128)(2,1)} %copy-done.12, bf16[128,3072]{1,0:T(8,128)(2,1)} %copy-done.11, bf16[128,3072]{1,0:T(8,128)(2,1)} %collective-permute-done.284.refs_3_, ...), custom_call_target="tpu_custom_call" | custom-call | flops 3221225472 | bytes 11534336 | tf_op jit(solution)/shard_map/student/pallas_call | solution.py:132
  60.0 0.0 copy-start.1
  60.0 0.0 collective-permute-done.288.refs_3_
  60.0 0.0 collective-permute-done.287.refs_2_
  60.0 0.0 collective-permute-done.286.refs_1_
  60.0 0.0 copy-start.6
  60.0 0.7 copy-done.6
  60.7 0.9 copy-done.7
  61.6 0.1 join.1.mine_ref
  61.7 8.9 %collective-permute-start.289 = (bf16[4,128,1024]{2,1,0:T(8,128)(2,1)S(1)}, bf16[4,128,1024]{2,1,0:T(8,128)(2,1)S(1)}, u32[]{:S(2)}, u32[]{:S(2)}) collective-permute-start(bf16[4,128,1024]{2,1,0:T(8,128)(2,1)S(1)} %join.1.mine_ref), channel_id=1, source_target_pairs={{0,1},{1,0},{2,3},{3,2},{4,5},{5,4},{6,7},{7,6},{8,9},{9,8},{10,11... | collective-permute-start | bytes 3145736 | tf_op jit(solution)/shard_map/ppermute | solution.py:19
  70.6 12.8 %all_to_all.10 = f32[32,1,640]{2,1,0:T(1,128)S(1)} all-to-all(f32[32,1,640]{2,1,0:T(1,128)} %get-tuple-element.595), channel_id=1, replica_groups=mesh['dp'=4,'vocab'=8] {'dp','vocab'}, dimensions={0} | all-to-all | bytes 163840 | tf_op jit(solution)/shard_map/all_to_all | solution.py:27
  83.4 0.0 collective-permute-done.289.got_ref
  83.4 0.0 copy-done.9
  83.4 0.0 copy-start
  83.5 1.6 %copy-done = f32[512,1024]{1,0:T(8,128)S(1)} copy-done((f32[512,1024]{1,0:T(8,128)S(1)}, f32[512,1024]{1,0:T(8,128)}, u32[]{:S(2)}) %copy-start) | copy-done | bytes 2097176
  85.0 2.4 %cross.1 = f32[32,1,1024]{2,1,0:T(1,128)} custom-call(s32[2]{0:T(128)S(1)} %copy-done.9, bf16[4,128,1024]{2,1,0:T(8,128)(2,1)S(1)} %join.1.mine_ref, bf16[4,128,1024]{2,1,0:T(8,128)(2,1)S(1)} %collective-permute-done.289.got_ref, f32[512,1024]{1,0:T(8,128)S(1)} %copy-done), custom_call_target="tpu_custom_call" | custom-call | flops 2621440 | bytes 4194304 | tf_op jit(solution)/shard_map/cross/pallas_call | solution.py:201
  87.5 1.1 copy-done.2
  88.6 2.6 %all-to-all-start.1 = ((f32[32,1,1024]{2,1,0:T(1,128)}), f32[32,1,1024]{2,1,0:T(1,128)S(1)}, u32[]{:S(2)}, u32[]{:S(2)}) async-start(f32[32,1,1024]{2,1,0:T(1,128)} %cross.1), calls=%async_computation.1 | async-start | bytes 262144 | tf_op jit(solution)/shard_map/all_to_all | solution.py:27
  91.2 0.1 fusion.8
  91.2 8.1 %all-to-all-done.1 = f32[32,1,1024]{2,1,0:T(1,128)S(1)} async-done(((f32[32,1,1024]{2,1,0:T(1,128)}), f32[32,1,1024]{2,1,0:T(1,128)S(1)}, u32[]{:S(2)}, u32[]{:S(2)}) %all-to-all-start.1) | async-done | bytes 131104 | tf_op jit(solution)/shard_map/all_to_all | solution.py:27
  99.4 0.6 subtract_add_fusion
  100.0 1.2 %copy-done.3 = bf16[4,128,1024]{2,1,0:T(8,128)(2,1)S(1)} copy-done((bf16[4,128,1024]{2,1,0:T(8,128)(2,1)S(1)}, bf16[4,128,1024]{2,1,0:T(8,128)(2,1)}, u32[]{:S(2)}) %copy-start.3) | copy-done | bytes 1048600
  101.2 1.8 %logit_grad.1.grad_ref = bf16[512,1024]{1,0:T(8,128)(2,1)S(1)} custom-call(s32[2]{0:T(128)S(1)} %copy-done.9, bf16[4,128,1024]{2,1,0:T(8,128)(2,1)S(1)} %join.1.mine_ref, bf16[4,128,1024]{2,1,0:T(8,128)(2,1)S(1)} %copy-done.3, f32[512,1024]{1,0:T(8,128)S(1)} %copy-done.1, f32[1,512]{1,0:T(1,128)S(1)} %bitcast.43, f32[1,512]{1,0:T(1,128)S(1)} %bitcast.42, ...), custom_call_target="tpu_custom_call" | custom-call | flops 2097152 | bytes 4194304 | tf_op jit(solution)/shard_map/logit_grad/pallas_call | solution.py:246
  103.0 1.1 copy-done.5
  104.1 7.4 %head_grad.1 = bf16[1,1024,3072]{2,1,0:T(8,128)(2,1)} custom-call(bf16[512,1024]{1,0:T(8,128)(2,1)} %copy-done.5, bf16[512,3072]{1,0:T(8,128)(2,1)} %get-tuple-element.596.hid_ref), custom_call_target="tpu_custom_call" | custom-call | flops 3221225472 | bytes 9437184 | tf_op jit(solution)/shard_map/head_grad/pallas_call | solution.py:271
  (16 shorter events, 0.1 us)
Async XLA Ops:
  0.6 6.8 %collective-permute-start.285 = (bf16[128,4096]{1,0:T(8,128)(2,1)}, bf16[128,4096]{1,0:T(8,128)(2,1)S(1)}, u32[]{:S(2)}, u32[]{:S(2)}) collective-permute-start(bf16[128,4096]{1,0:T(8,128)(2,1)} %refs_5_.1), channel_id=1, source_target_pairs={{0,1},{1,0},{2,3},{3,2},{4,5},{5,4},{6,7},{7,6},{8,9},{9,8},{10,11... | collective-permute-start | bytes 3145736 | tf_op jit(solution)/shard_map/ppermute | solution.py:19
  1.1 43.5 %collective-permute-start.283 = (bf16[128,3072]{1,0:T(8,128)(2,1)}, bf16[128,3072]{1,0:T(8,128)(2,1)S(1)}, u32[]{:S(2)}, u32[]{:S(2)}) collective-permute-start(bf16[128,3072]{1,0:T(8,128)(2,1)} %refs_0_), channel_id=1, source_target_pairs={{0,16},{8,24},{16,0},{24,8},{1,17},{9,25},{17,1},{25,9},{2,18},{10... | collective-permute-start | bytes 2359304 | tf_op jit(solution)/shard_map/ppermute | solution.py:19
  3.7 41.0 %collective-permute-start.282 = (bf16[128,3072]{1,0:T(8,128)(2,1)}, bf16[128,3072]{1,0:T(8,128)(2,1)S(1)}, u32[]{:S(2)}, u32[]{:S(2)}) collective-permute-start(bf16[128,3072]{1,0:T(8,128)(2,1)} %refs_0_), channel_id=1, source_target_pairs={{0,8},{8,0},{16,24},{24,16},{1,9},{9,1},{17,25},{25,17},{2,10},{10... | collective-permute-start | bytes 2359304 | tf_op jit(solution)/shard_map/ppermute | solution.py:19
  5.2 39.5 %collective-permute-start.284 = (bf16[128,3072]{1,0:T(8,128)(2,1)}, bf16[128,3072]{1,0:T(8,128)(2,1)}, u32[]{:S(2)}, u32[]{:S(2)}) collective-permute-start(bf16[128,3072]{1,0:T(8,128)(2,1)} %refs_0_), channel_id=1, source_target_pairs={{0,24},{8,16},{16,8},{24,0},{1,25},{9,17},{17,9},{25,1},{2,26},{10... | collective-permute-start | bytes 2359304 | tf_op jit(solution)/shard_map/ppermute | solution.py:19
  7.5 1.2 %copy-start.4 = (bf16[128,4096]{1,0:T(8,128)(2,1)S(1)}, bf16[128,4096]{1,0:T(8,128)(2,1)}, u32[]{:S(2)}) copy-start(bf16[128,4096]{1,0:T(8,128)(2,1)} %refs_5_.1) | copy-start | bytes 3145732
  8.7 0.7 copy-start.8
  10.1 34.6 %collective-permute-start.76 = (bf16[4,128,1024]{2,1,0:T(8,128)(2,1)S(1)}, bf16[4,128,1024]{2,1,0:T(8,128)(2,1)}, u32[]{:S(2)}, u32[]{:S(2)}) collective-permute-start(bf16[4,128,1024]{2,1,0:T(8,128)(2,1)S(1)} %param.76), channel_id=1, source_target_pairs={{0,4},{1,7},{2,6},{3,3},{4,2},{5,1},{6,0},{7,5},{8,12},{9,15},{10,... | collective-permute-start | bytes 3145736 | tf_op jit(solution)/shard_map/cond/branch_76_fun/ppermute | solution.py:424
  44.7 5.4 %copy-start.11 = (bf16[128,3072]{1,0:T(8,128)(2,1)}, bf16[128,3072]{1,0:T(8,128)(2,1)S(1)}, u32[]{:S(2)}) copy-start(bf16[128,3072]{1,0:T(8,128)(2,1)S(1)} %collective-permute-done.283.refs_2_) | copy-start | bytes 2359300
  44.7 5.4 %copy-start.12 = (bf16[128,3072]{1,0:T(8,128)(2,1)}, bf16[128,3072]{1,0:T(8,128)(2,1)S(1)}, u32[]{:S(2)}) copy-start(bf16[128,3072]{1,0:T(8,128)(2,1)S(1)} %collective-permute-done.282.refs_1_) | copy-start | bytes 2359300
  46.5 13.4 %collective-permute-start.288 = (bf16[128,1024]{1,0:T(8,128)(2,1)S(1)}, bf16[128,1024]{1,0:T(8,128)(2,1)S(1)}, u32[]{:S(2)}, u32[]{:S(2)}) collective-permute-start(bf16[128,1024]{1,0:T(8,128)(2,1)S(1)} %get-tuple-element.599), channel_id=1, source_target_pairs={{0,24},{8,16},{16,8},{24,0},{1,25},{9,17},{17,9},{25,1},{2,26},{10... | collective-permute-start | bytes 786440 | tf_op jit(solution)/shard_map/ppermute | solution.py:19
  49.0 11.0 %collective-permute-start.287 = (bf16[128,1024]{1,0:T(8,128)(2,1)S(1)}, bf16[128,1024]{1,0:T(8,128)(2,1)S(1)}, u32[]{:S(2)}, u32[]{:S(2)}) collective-permute-start(bf16[128,1024]{1,0:T(8,128)(2,1)S(1)} %get-tuple-element.600), channel_id=1, source_target_pairs={{0,16},{8,24},{16,0},{24,8},{1,17},{9,25},{17,1},{25,9},{2,18},{10... | collective-permute-start | bytes 786440 | tf_op jit(solution)/shard_map/ppermute | solution.py:19
  49.5 33.9 %copy-start.9 = (s32[2]{0:T(128)S(1)}, s32[2]{0:T(128)}, u32[]{:S(2)}) copy-start(s32[2]{0:T(128)} %get-tuple-element.582.flags_ref) | copy-start | bytes 28
  49.5 10.4 %collective-permute-start.286 = (bf16[128,1024]{1,0:T(8,128)(2,1)S(1)}, bf16[128,1024]{1,0:T(8,128)(2,1)S(1)}, u32[]{:S(2)}, u32[]{:S(2)}) collective-permute-start(bf16[128,1024]{1,0:T(8,128)(2,1)S(1)} %get-tuple-element.601), channel_id=1, source_target_pairs={{0,8},{8,0},{16,24},{24,16},{1,9},{9,1},{17,25},{25,17},{2,10},{10... | collective-permute-start | bytes 786440 | tf_op jit(solution)/shard_map/ppermute | solution.py:19
  50.1 49.9 %copy-start.10 = (f32[512]{0:T(512)S(1)}, f32[512]{0:T(512)}, u32[]{:S(2)}) copy-start(f32[512]{0:T(512)} %param.293) | copy-start | bytes 6148
  60.0 40.0 %copy-start.1 = (f32[512,1024]{1,0:T(8,128)S(1)}, f32[512,1024]{1,0:T(8,128)}, u32[]{:S(2)}) copy-start(f32[512,1024]{1,0:T(8,128)} %get-tuple-element.594.scores_ref) | copy-start | bytes 6291460
  60.0 0.7 copy-start.6
  60.7 0.9 copy-start.7
  61.7 21.7 %collective-permute-start.289 = (bf16[4,128,1024]{2,1,0:T(8,128)(2,1)S(1)}, bf16[4,128,1024]{2,1,0:T(8,128)(2,1)S(1)}, u32[]{:S(2)}, u32[]{:S(2)}) collective-permute-start(bf16[4,128,1024]{2,1,0:T(8,128)(2,1)S(1)} %join.1.mine_ref), channel_id=1, source_target_pairs={{0,1},{1,0},{2,3},{3,2},{4,5},{5,4},{6,7},{7,6},{8,9},{9,8},{10,11... | collective-permute-start | bytes 3145736 | tf_op jit(solution)/shard_map/ppermute | solution.py:19
  83.4 1.6 %copy-start = (f32[512,1024]{1,0:T(8,128)S(1)}, f32[512,1024]{1,0:T(8,128)}, u32[]{:S(2)}) copy-start(f32[512,1024]{1,0:T(8,128)} %get-tuple-element.594.scores_ref) | copy-start | bytes 6291460
  87.5 1.1 copy-start.2
  88.6 10.7 %all-to-all-start.1 = ((f32[32,1,1024]{2,1,0:T(1,128)}), f32[32,1,1024]{2,1,0:T(1,128)S(1)}, u32[]{:S(2)}, u32[]{:S(2)}) async-start(f32[32,1,1024]{2,1,0:T(1,128)} %cross.1), calls=%async_computation.1 | async-start | bytes 262144 | tf_op jit(solution)/shard_map/all_to_all | solution.py:27
  100.0 1.2 %copy-start.3 = (bf16[4,128,1024]{2,1,0:T(8,128)(2,1)S(1)}, bf16[4,128,1024]{2,1,0:T(8,128)(2,1)}, u32[]{:S(2)}) copy-start(bf16[4,128,1024]{2,1,0:T(8,128)(2,1)} %copy-done.2) | copy-start | bytes 3145732
  103.0 1.1 copy-start.5

commit v3 on v2

--- a/solution.py
+++ b/solution.py
@@ -213,78 +213,98 @@
     )(flags, mine, got, scores)
 
 
-def logit_grad_kernel(
-    flags_ref, mine_ref, got_ref, scores_ref, row_s_ref, row_t_ref, weight_ref, grad_ref, col_ref
+def head_grad_kernel(
+    flags_ref, mine_ref, got_ref, scores_in_ref, hid_in_ref, row_s_ref, row_t_ref, weight_ref, out_ref,
+    target_ref, scores_ref, hid_ref, grad_ref, col_ref, target_sems, scores_sems, hid_sem,
 ):
+    n_dp, rows, _ = target_ref.shape
+    tokens = n_dp * rows
+    block = out_ref.shape[1]
     step = pl.program_id(0)
-    rows = scores_ref.shape[0]
-    tokens = col_ref.shape[0]
-    half = rows // 2
-    at = place(rows)(step)
 
     @pl.when(step == 0)
     def _():
+        at = place(rows)
+        half = rows // 2
+        hid_copy = pltpu.make_async_copy(hid_in_ref, hid_ref, hid_sem)
+
+        def target_copy(ref, k):
+            return pltpu.make_async_copy(ref.at[k], target_ref.at[k], target_sems.at[k])
+
+        def scores_copy(k):
+            here = pl.ds(pl.multiple_of(k * rows, rows), rows)
+            return pltpu.make_async_copy(
+                scores_in_ref.at[here], scores_ref.at[here], scores_sems.at[k]
+            )
+
+        for k in range(n_dp):
+            scores_copy(k).start()
+
+            @pl.when(flags_ref[1] != 0)
+            def _():
+                target_copy(mine_ref, k).start()
+
+            @pl.when(flags_ref[1] == 0)
+            def _():
+                target_copy(got_ref, k).start()
+
+        hid_copy.start()
         line = lax.broadcasted_iota(jnp.int32, (128, tokens), 0)
         col_ref[...] = jnp.transpose(
             jnp.where(line == 0, row_s_ref[...], jnp.where(line == 1, row_t_ref[...], weight_ref[...]))
         )
 
-    keep = flags_ref[1] != 0
-    for first in (0, half):
-        part = slice(first, first + half)
-        cols = col_ref[pl.ds(pl.multiple_of(at + first, half), half)]
-        target = jnp.where(keep, mine_ref[0, part], got_ref[0, part]).astype(jnp.float32)
-        prob_s = jnp.exp(scores_ref[part] - cols[:, 0:1])
-        prob_t = jnp.exp(target - cols[:, 1:2])
-        grad_ref[part] = (cols[:, 2:3] * (prob_s - prob_t)).astype(jnp.bfloat16)
-
-
-def logit_grad_call(flags, mine, got, scores, total_s, total_t, weight):
+        def piece(k, carry):
+            scores_copy(k).wait()
+            target_copy(mine_ref, k).wait()
+            for first in (0, half):
+                part = pl.ds(pl.multiple_of(k * rows + first, half), half)
+                cols = col_ref[pl.ds(pl.multiple_of(at(k) + first, half), half)]
+                target = target_ref[k, first : first + half].astype(jnp.float32)
+                prob_s = jnp.exp(scores_ref[part] - cols[:, 0:1])
+                prob_t = jnp.exp(target - cols[:, 1:2])
+                grad_ref[part] = (cols[:, 2:3] * (prob_s - prob_t)).astype(jnp.bfloat16)
+            return carry
+
+        lax.fori_loop(0, n_dp, piece, 0)
+        hid_copy.wait()
+
+    ids = pl.ds(pl.multiple_of(step * block, block), block)
+    out_ref[0] = lax.dot_general(
+        grad_ref[:, ids], hid_ref[...], (((0,), (0,)), ((), ())), preferred_element_type=jnp.float32
+    ).astype(jnp.bfloat16)
+
+
+def head_grad_call(flags, mine, got, scores, hid, total_s, total_t, weight):
     n_dp, part, rows = mine.shape
-    tokens = n_dp * part
-    whole_row = pl.BlockSpec((1, tokens), lambda k: (0, 0))
-    return pl.pallas_call(
-        logit_grad_kernel,
-        grid=(n_dp,),
-        in_specs=block_specs(n_dp, part, rows) + [whole_row] * 3,
-        out_specs=pl.BlockSpec((part, rows), lambda k: (k, 0)),
-        out_shape=jax.ShapeDtypeStruct((tokens, rows), jnp.bfloat16),
-        scratch_shapes=[pltpu.VMEM((tokens, 128), jnp.float32)],
-        compiler_params=pltpu.CompilerParams(vmem_limit_bytes=24 * MIB),
-        cost_estimate=pl.CostEstimate(
-            flops=4 * tokens * rows, bytes_accessed=8 * tokens * rows, transcendentals=2 * tokens * rows
-        ),
-        name="logit_grad",
-    )(flags, mine, got, scores, total_s[None], total_t[None], weight[None])
-
-
-def head_grad_kernel(grad_ref, hid_ref, out_ref):
-    out_ref[0] = lax.dot_general(
-        grad_ref[...], hid_ref[...], (((0,), (0,)), ((), ())), preferred_element_type=jnp.float32
-    ).astype(jnp.bfloat16)
-
-
-def head_grad_call(logit_grad, hid):
-    tokens, rows = logit_grad.shape
-    depth = hid.shape[1]
+    tokens, depth = hid.shape
     block = min(256, rows)
+    in_hbm = pl.BlockSpec(memory_space=pltpu.HBM)
+    whole_row = pl.BlockSpec((1, tokens), lambda i: (0, 0))
     return pl.pallas_call(
         head_grad_kernel,
         grid=(rows // block,),
-        in_specs=[
-            pl.BlockSpec((tokens, block), lambda i: (0, i)),
-            pl.BlockSpec((tokens, depth), lambda i: (0, 0)),
-        ],
+        in_specs=[pl.BlockSpec(memory_space=pltpu.SMEM)] + [in_hbm] * 4 + [whole_row] * 3,
         out_specs=pl.BlockSpec((1, block, depth), lambda i: (0, i, 0)),
         out_shape=jax.ShapeDtypeStruct((1, rows, depth), jnp.bfloat16),
+        scratch_shapes=[
+            pltpu.VMEM(mine.shape, jnp.bfloat16),
+            pltpu.VMEM((tokens, rows), jnp.float32),
+            pltpu.VMEM((tokens, depth), jnp.bfloat16),
+            pltpu.VMEM((tokens, rows), jnp.bfloat16),
+            pltpu.VMEM((tokens, 128), jnp.float32),
+            pltpu.SemaphoreType.DMA((n_dp,)),
+            pltpu.SemaphoreType.DMA((n_dp,)),
+            pltpu.SemaphoreType.DMA,
+        ],
         compiler_params=pltpu.CompilerParams(vmem_limit_bytes=60 * MIB),
         cost_estimate=pl.CostEstimate(
             flops=2 * tokens * rows * depth,
-            bytes_accessed=2 * rows * depth + 2 * tokens * depth,
-            transcendentals=0,
+            bytes_accessed=2 * rows * depth + 2 * tokens * depth + 6 * tokens * rows,
+            transcendentals=2 * tokens * rows,
         ),
         name="head_grad",
-    )(logit_grad, hid)
+    )(flags, mine, got, scores, hid, total_s[None], total_t[None], weight[None])
 
 
 def chip_plans(n):
@@ -444,10 +464,11 @@
         )
         flags, got = jnp.ones((2,), jnp.int32), mine
 
-    total_s, total_t = combine_stats(exchange(stats), tokens)
-    parts = exchange(cross_call(flags, mine, got, student))
-    logit_grad = logit_grad_call(flags, mine, got, student, total_s, total_t, loss_weight)
-    head_grad = head_grad_call(logit_grad, hid)
+    sent = cross_call(flags, mine, got, student)
+    parts, sent = lax.optimization_barrier((exchange(stats), sent))
+    total_s, total_t = combine_stats(parts, tokens)
+    head_grad = head_grad_call(flags, mine, got, student, hid, total_s, total_t, loss_weight)
+    parts, head_grad = lax.optimization_barrier((exchange(sent), head_grad))
     tops, terms = parts[:, 0, :tokens], parts[:, 0, tokens:]
     divergence = jnp.sum(terms * jnp.exp(tops - total_t), axis=0) - total_t + total_s
     return head_grad, divergence

time: 111 us -> 84.3 us (0.76); the launches traced: 112 us -> 83.5 us
  blocking collectives: 12.8 us -> 0 us
  waiting for transfers between devices: 35.4 us -> 27.6 us
  local copies, waits for them, and re-layouts: 10.4 us -> 5.12 us
  starting transfers between devices: 27 us -> 23.4 us
  other arithmetic: 0.78 us -> 1.93 us
    ppermute x1, waiting for transfers between devices: 27.3 us -> 0.01 us  [over_chips(): return lax.ppermute(x, 'vocab', pairs)]
    ppermute x8, waiting for transfers between devices: 0.02 us -> 24.5 us  [xor_permute(): return lax.ppermute(x, axis, [(i, i ^ k) for i in range(size)])]
    all_to_all x1 -> x0, blocking collectives: 12.8 us -> none  [exchange(): lax.all_to_all(copies, ('dp', 'vocab'), split_axis=0, concat_axis=0, tile...]
    ppermute x8, starting transfers between devices: 17.1 us -> 8.62 us  [xor_permute(): return lax.ppermute(x, axis, [(i, i ^ k) for i in range(size)])]
    all_to_all x1 -> x2, waiting for transfers between devices: 8.07 us -> 3.16 us  [exchange(): lax.all_to_all(copies, ('dp', 'vocab'), split_axis=0, concat_axis=0, tile...]
    unnamed x26 -> x18, local copies, waits for them, and re-layouts: 8.52 us -> 3.81 us
    all_to_all x1 -> x2, starting transfers between devices: 2.56 us -> 7.04 us  [exchange(): lax.all_to_all(copies, ('dp', 'vocab'), split_axis=0, concat_axis=0, tile...]
    pallas_call x1 -> x0, Pallas kernels: 1.78 us -> none  [logit_grad_call(): pl.pallas_call(logit_grad_kernel, grid=(n_dp,), in_specs=block_specs(n_dp...]
  transfers between devices with their start and end apart: 10 -> 11, of which waited for: 2 -> 5; matrix products, arithmetic and copies ran while one was open for 0% -> 1% of each run, Pallas kernels for 11% -> 28%
where the time goes in v3:
time: 84.3 us; the launch traced here: 83.5 us
  waiting for transfers between devices  27.6 us (33%)
  Pallas kernels  23.7 us (28%)
  starting transfers between devices  23.4 us (28%)
  local copies, waits for them, and re-layouts  5.12 us (6%)
  other arithmetic  1.93 us (2%)
  between operations  1.47 us (2%)
    ppermute x8, waiting for transfers between devices, xor_permute(): return lax.ppermute(x, axis, [(i, i ^ k) for i in range(size)])  24.5 us
    pallas_call x1, Pallas kernels, student_call(): pl.pallas_call(functools.partial(student_kernel, len(chunks)), in_specs=[...  9.93 us
    pallas_call x1, Pallas kernels, head_grad_call(): pl.pallas_call(head_grad_kernel, grid=(rows // block,), in_specs=[pl.Bloc...  9.17 us
    ppermute x8, starting transfers between devices, xor_permute(): return lax.ppermute(x, axis, [(i, i ^ k) for i in range(size)])  8.62 us
    ppermute x1, starting transfers between devices, over_chips(): return lax.ppermute(x, 'vocab', pairs)  7.71 us
    all_to_all x2, starting transfers between devices, exchange(): lax.all_to_all(copies, ('dp', 'vocab'), split_axis=0, concat_axis=0, tile...  7.04 us
    unnamed x18, local copies, waits for them, and re-layouts  3.81 us
    all_to_all x2, waiting for transfers between devices, exchange(): lax.all_to_all(copies, ('dp', 'vocab'), split_axis=0, concat_axis=0, tile...  3.16 us
  transfers between devices with their start and end apart: 11, of which 5 were waited for; matrix products, arithmetic and copies ran while one was open for 1% of the time, Pallas kernels for 28%

profile of v3, /device:TPU:0, one launch (start us, length us, event | category | flops | bytes accessed | tf_op | source)
XLA Modules:
  0.0 83.5 jit_solution(13882937506897081082)
XLA Ops:
  0.6 0.5 collective-permute-start.285
  1.1 2.6 %collective-permute-start.283 = (bf16[128,3072]{1,0:T(8,128)(2,1)}, bf16[128,3072]{1,0:T(8,128)(2,1)S(1)}, u32[]{:S(2)}, u32[]{:S(2)}) collective-permute-start(bf16[128,3072]{1,0:T(8,128)(2,1)} %refs_0_), channel_id=1, source_target_pairs={{0,16},{8,24},{16,0},{24,8},{1,17},{9,25},{17,1},{25,9},{2,18},{10... | collective-permute-start | bytes 2359304 | tf_op jit(solution)/shard_map/ppermute | solution.py:19
  3.7 1.5 %collective-permute-start.282 = (bf16[128,3072]{1,0:T(8,128)(2,1)}, bf16[128,3072]{1,0:T(8,128)(2,1)}, u32[]{:S(2)}, u32[]{:S(2)}) collective-permute-start(bf16[128,3072]{1,0:T(8,128)(2,1)} %refs_0_), channel_id=1, source_target_pairs={{0,8},{8,0},{16,24},{24,16},{1,9},{9,1},{17,25},{25,17},{2,10},{10... | collective-permute-start | bytes 2359304 | tf_op jit(solution)/shard_map/ppermute | solution.py:19
  5.2 0.1 collective-permute-start.284
  5.3 1.5 %plan.1 = (s32[1]{0:T(128)}, s32[2]{0:T(128)}) custom-call(s32[8]{0:T(128)} %order_ref.1, s32[8,128]{1,0:T(8,128)} %constant.14.clone.codes_ref, s32[8,128]{1,0:T(8,128)} %constant.15.clone.keys_ref), custom_call_target="tpu_custom_call" | custom-call | tf_op jit(solution)/shard_map/plan/pallas_call | solution.py:362
  7.4 0.0 collective-permute-done.285.other_ref
  7.5 0.0 copy-start.3
  7.5 1.2 %copy-done.3 = bf16[128,4096]{1,0:T(8,128)(2,1)S(1)} copy-done((bf16[128,4096]{1,0:T(8,128)(2,1)S(1)}, bf16[128,4096]{1,0:T(8,128)(2,1)}, u32[]{:S(2)}) %copy-start.3) | copy-done | bytes 1048600
  8.7 0.0 copy-start.4
  8.7 0.6 copy-done.4
  9.3 0.7 pick.1
  10.0 7.9 %conditional.1 = (bf16[4,128,1024]{2,1,0:T(8,128)(2,1)}) conditional(s32[]{:T(128)} %bitcast, bf16[4,128,1024]{2,1,0:T(8,128)(2,1)S(1)} %pick.1, bf16[4,128,1024]{2,1,0:T(8,128)(2,1)S(1)} %pick.1, bf16[4,128,1024]{2,1,0:T(8,128)(2,1)S(1)} %pick.1, bf16[4,128,1024]{2,1,0:T(8,128)(2,1)S(1)} %pick.1, ...), branch_computations={%region_0.0_spmd, %region_1.0_spmd, %region_2.0_spmd, %region_3.0_... | conditional | bytes 4194352 | solution.py:446
  10.2 7.7 %collective-permute-start.234 = (bf16[4,128,1024]{2,1,0:T(8,128)(2,1)S(1)}, bf16[4,128,1024]{2,1,0:T(8,128)(2,1)}, u32[]{:S(2)}, u32[]{:S(2)}) collective-permute-start(bf16[4,128,1024]{2,1,0:T(8,128)(2,1)S(1)} %param.234), channel_id=1, source_target_pairs={{0,0},{1,7},{2,4},{3,3},{4,2},{5,1},{6,6},{7,5},{8,8},{9,15},{10,1... | collective-permute-start | bytes 3145736 | tf_op jit(solution)/shard_map/cond/branch_234_fun/ppermute | solution.py:444
  17.9 0.0 collective-permute-done.234
  17.9 4.2 %collective-permute-done.283.refs_2_ = bf16[128,3072]{1,0:T(8,128)(2,1)S(1)} collective-permute-done((bf16[128,3072]{1,0:T(8,128)(2,1)}, bf16[128,3072]{1,0:T(8,128)(2,1)S(1)}, u32[]{:S(2)}, u32[]{:S(2)}) %collective-permute-start.283) | collective-permute-done | bytes 786464 | tf_op jit(solution)/shard_map/ppermute | solution.py:19
  22.1 2.4 %collective-permute-done.282.refs_1_ = bf16[128,3072]{1,0:T(8,128)(2,1)} collective-permute-done((bf16[128,3072]{1,0:T(8,128)(2,1)}, bf16[128,3072]{1,0:T(8,128)(2,1)}, u32[]{:S(2)}, u32[]{:S(2)}) %collective-permute-start.282) | collective-permute-done | bytes 786464 | tf_op jit(solution)/shard_map/ppermute | solution.py:19
  24.4 15.8 %collective-permute-done.284.refs_3_ = bf16[128,3072]{1,0:T(8,128)(2,1)} collective-permute-done((bf16[128,3072]{1,0:T(8,128)(2,1)}, bf16[128,3072]{1,0:T(8,128)(2,1)}, u32[]{:S(2)}, u32[]{:S(2)}) %collective-permute-start.284) | collective-permute-done | bytes 786464 | tf_op jit(solution)/shard_map/ppermute | solution.py:19
  40.2 1.3 %slice_bitcast_fusion = (bf16[128,1024]{1,0:T(8,128)(2,1)S(1)}, bf16[128,1024]{1,0:T(8,128)(2,1)S(1)}, bf16[128,1024]{1,0:T(8,128)(2,1)S(1)}, bf16[128,1024]{1,0:T(8,128)(2,1)S(1)}) fusion(bf16[4,128,1024]{2,1,0:T(8,128)(2,1)} %get-tuple-element.611), kind=kLoop, calls=%fused_computation | loop fusion | bytes 2097152 | tf_op jit(solution)/shard_map/squeeze | solution.py:452
  41.5 2.7 %collective-permute-start.288 = (bf16[128,1024]{1,0:T(8,128)(2,1)S(1)}, bf16[128,1024]{1,0:T(8,128)(2,1)S(1)}, u32[]{:S(2)}, u32[]{:S(2)}) collective-permute-start(bf16[128,1024]{1,0:T(8,128)(2,1)S(1)} %get-tuple-element.605), channel_id=1, source_target_pairs={{0,24},{8,16},{16,8},{24,0},{1,25},{9,17},{17,9},{25,1},{2,26},{10... | collective-permute-start | bytes 786440 | tf_op jit(solution)/shard_map/ppermute | solution.py:19
  44.2 0.5 collective-permute-start.287
  44.7 0.3 collective-permute-start.286
  45.1 0.0 copy-done.8
  45.1 9.9 %student.1 = (f32[512,1024]{1,0:T(8,128)}, bf16[512,3072]{1,0:T(8,128)(2,1)}, f32[32,1,640]{2,1,0:T(1,128)}) custom-call(bf16[128,3072]{1,0:T(8,128)(2,1)} %refs_0_, bf16[128,3072]{1,0:T(8,128)(2,1)} %collective-permute-done.282.refs_1_, bf16[128,3072]{1,0:T(8,128)(2,1)} %copy-done.8, bf16[128,3072]{1,0:T(8,128)(2,1)} %collective-permute-done.284.refs_3_, ...), custom_call_target="tpu_custom_call" | custom-call | flops 3221225472 | bytes 11534336 | tf_op jit(solution)/shard_map/student/pallas_call | solution.py:132
  55.0 0.0 collective-permute-done.288.refs_3_
  55.0 2.1 %collective-permute-done.287.refs_2_ = bf16[128,1024]{1,0:T(8,128)(2,1)S(1)} collective-permute-done((bf16[128,1024]{1,0:T(8,128)(2,1)S(1)}, bf16[128,1024]{1,0:T(8,128)(2,1)S(1)}, u32[]{:S(2)}, u32[]{:S(2)}) %collective-permute-start.287) | collective-permute-done | bytes 262176 | tf_op jit(solution)/shard_map/ppermute | solution.py:19
  57.1 0.0 collective-permute-done.286.refs_1_
  57.1 0.1 join.1.mine_ref
  57.2 0.0 copy-start
  57.2 0.4 collective-permute-start.289
  57.6 4.4 %all-to-all-start = ((f32[32,1,640]{2,1,0:T(1,128)}), f32[32,1,640]{2,1,0:T(1,128)S(1)}, u32[]{:S(2)}, u32[]{:S(2)}) async-start(f32[32,1,640]{2,1,0:T(1,128)} %get-tuple-element.594), calls=%async_computation | async-start | bytes 163840 | tf_op jit(solution)/shard_map/all_to_all | solution.py:27
  62.0 0.0 collective-permute-done.289.got_ref
  62.0 0.0 copy-start.2
  62.0 0.0 copy-done.5
  62.0 0.0 copy-start.1
  62.0 2.0 %copy-done.1 = f32[512,1024]{1,0:T(8,128)S(1)} copy-done((f32[512,1024]{1,0:T(8,128)S(1)}, f32[512,1024]{1,0:T(8,128)}, u32[]{:S(2)}) %copy-start.1) | copy-done | bytes 2097176
  64.0 2.4 %cross.1 = f32[32,1,1024]{2,1,0:T(1,128)} custom-call(s32[2]{0:T(128)S(1)} %copy-done.5, bf16[4,128,1024]{2,1,0:T(8,128)(2,1)S(1)} %join.1.mine_ref, bf16[4,128,1024]{2,1,0:T(8,128)(2,1)S(1)} %collective-permute-done.289.got_ref, f32[512,1024]{1,0:T(8,128)S(1)} %copy-done.1), custom_call_target="tpu_custom_call" | custom-call | flops 2621440 | bytes 4194304 | tf_op jit(solution)/shard_map/cross/pallas_call | solution.py:201
  66.4 3.2 %all-to-all-done = f32[32,1,640]{2,1,0:T(1,128)S(1)} async-done(((f32[32,1,640]{2,1,0:T(1,128)}), f32[32,1,640]{2,1,0:T(1,128)S(1)}, u32[]{:S(2)}, u32[]{:S(2)}) %all-to-all-start) | async-done | bytes 81952 | tf_op jit(solution)/shard_map/all_to_all | solution.py:27
  69.6 0.1 fusion.7
  69.7 2.7 %all-to-all-start.1 = ((f32[32,1,1024]{2,1,0:T(1,128)}), f32[32,1,1024]{2,1,0:T(1,128)S(1)}, u32[]{:S(2)}, u32[]{:S(2)}) async-start(f32[32,1,1024]{2,1,0:T(1,128)} %cross.1), calls=%async_computation.1 | async-start | bytes 262144 | tf_op jit(solution)/shard_map/all_to_all | solution.py:27
  72.4 0.6 log_add_fusion.1
  73.0 0.6 log_add_fusion
  73.6 0.0 copy-done
  73.6 0.0 copy-done.2
  73.6 9.2 %head_grad.1 = bf16[1,1024,3072]{2,1,0:T(8,128)(2,1)} custom-call(s32[2]{0:T(128)} %get-tuple-element.587.flags_ref, bf16[4,128,1024]{2,1,0:T(8,128)(2,1)} %copy-done, bf16[4,128,1024]{2,1,0:T(8,128)(2,1)} %copy-done.2, f32[512,1024]{1,0:T(8,128)} %get-tuple-element.599.scores_ref.scores_in_ref, bf16[512,3072]{1,0:T(8,128)(2,1)} %get-tuple-element.601.hid_in_ref, ...), custom_call_target="tpu_custom_call" | custom-call | flops 3221225472 | bytes 12582912 | tf_op jit(solution)/shard_map/head_grad/pallas_call | solution.py:284
  82.8 0.0 all-to-all-done.1
  82.8 0.0 copy-done.6
  82.9 0.0 copy-done.7
  82.9 0.6 subtract_add_fusion
  (11 shorter events, 0.2 us)
Async XLA Ops:
  0.6 6.8 %collective-permute-start.285 = (bf16[128,4096]{1,0:T(8,128)(2,1)}, bf16[128,4096]{1,0:T(8,128)(2,1)S(1)}, u32[]{:S(2)}, u32[]{:S(2)}) collective-permute-start(bf16[128,4096]{1,0:T(8,128)(2,1)} %refs_5_.1), channel_id=1, source_target_pairs={{0,1},{1,0},{2,3},{3,2},{4,5},{5,4},{6,7},{7,6},{8,9},{9,8},{10,11... | collective-permute-start | bytes 3145736 | tf_op jit(solution)/shard_map/ppermute | solution.py:19
  1.1 20.9 %collective-permute-start.283 = (bf16[128,3072]{1,0:T(8,128)(2,1)}, bf16[128,3072]{1,0:T(8,128)(2,1)S(1)}, u32[]{:S(2)}, u32[]{:S(2)}) collective-permute-start(bf16[128,3072]{1,0:T(8,128)(2,1)} %refs_0_), channel_id=1, source_target_pairs={{0,16},{8,24},{16,0},{24,8},{1,17},{9,25},{17,1},{25,9},{2,18},{10... | collective-permute-start | bytes 2359304 | tf_op jit(solution)/shard_map/ppermute | solution.py:19
  3.7 20.7 %collective-permute-start.282 = (bf16[128,3072]{1,0:T(8,128)(2,1)}, bf16[128,3072]{1,0:T(8,128)(2,1)}, u32[]{:S(2)}, u32[]{:S(2)}) collective-permute-start(bf16[128,3072]{1,0:T(8,128)(2,1)} %refs_0_), channel_id=1, source_target_pairs={{0,8},{8,0},{16,24},{24,16},{1,9},{9,1},{17,25},{25,17},{2,10},{10... | collective-permute-start | bytes 2359304 | tf_op jit(solution)/shard_map/ppermute | solution.py:19
  5.2 35.0 %collective-permute-start.284 = (bf16[128,3072]{1,0:T(8,128)(2,1)}, bf16[128,3072]{1,0:T(8,128)(2,1)}, u32[]{:S(2)}, u32[]{:S(2)}) collective-permute-start(bf16[128,3072]{1,0:T(8,128)(2,1)} %refs_0_), channel_id=1, source_target_pairs={{0,24},{8,16},{16,8},{24,0},{1,25},{9,17},{17,9},{25,1},{2,26},{10... | collective-permute-start | bytes 2359304 | tf_op jit(solution)/shard_map/ppermute | solution.py:19
  7.5 1.2 %copy-start.3 = (bf16[128,4096]{1,0:T(8,128)(2,1)S(1)}, bf16[128,4096]{1,0:T(8,128)(2,1)}, u32[]{:S(2)}) copy-start(bf16[128,4096]{1,0:T(8,128)(2,1)} %refs_5_.1) | copy-start | bytes 3145732
  8.7 0.6 copy-start.4
  10.2 7.7 %collective-permute-start.234 = (bf16[4,128,1024]{2,1,0:T(8,128)(2,1)S(1)}, bf16[4,128,1024]{2,1,0:T(8,128)(2,1)}, u32[]{:S(2)}, u32[]{:S(2)}) collective-permute-start(bf16[4,128,1024]{2,1,0:T(8,128)(2,1)S(1)} %param.234), channel_id=1, source_target_pairs={{0,0},{1,7},{2,4},{3,3},{4,2},{5,1},{6,6},{7,5},{8,8},{9,15},{10,1... | collective-permute-start | bytes 3145736 | tf_op jit(solution)/shard_map/cond/branch_234_fun/ppermute | solution.py:444
  22.1 23.0 %copy-start.8 = (bf16[128,3072]{1,0:T(8,128)(2,1)}, bf16[128,3072]{1,0:T(8,128)(2,1)S(1)}, u32[]{:S(2)}) copy-start(bf16[128,3072]{1,0:T(8,128)(2,1)S(1)} %collective-permute-done.283.refs_2_) | copy-start | bytes 2359300
  41.5 13.5 %collective-permute-start.288 = (bf16[128,1024]{1,0:T(8,128)(2,1)S(1)}, bf16[128,1024]{1,0:T(8,128)(2,1)S(1)}, u32[]{:S(2)}, u32[]{:S(2)}) collective-permute-start(bf16[128,1024]{1,0:T(8,128)(2,1)S(1)} %get-tuple-element.605), channel_id=1, source_target_pairs={{0,24},{8,16},{16,8},{24,0},{1,25},{9,17},{17,9},{25,1},{2,26},{10... | collective-permute-start | bytes 786440 | tf_op jit(solution)/shard_map/ppermute | solution.py:19
  44.2 12.9 %collective-permute-start.287 = (bf16[128,1024]{1,0:T(8,128)(2,1)S(1)}, bf16[128,1024]{1,0:T(8,128)(2,1)S(1)}, u32[]{:S(2)}, u32[]{:S(2)}) collective-permute-start(bf16[128,1024]{1,0:T(8,128)(2,1)S(1)} %get-tuple-element.606), channel_id=1, source_target_pairs={{0,16},{8,24},{16,0},{24,8},{1,17},{9,25},{17,1},{25,9},{2,18},{10... | collective-permute-start | bytes 786440 | tf_op jit(solution)/shard_map/ppermute | solution.py:19
  44.7 17.3 %copy-start.5 = (s32[2]{0:T(128)S(1)}, s32[2]{0:T(128)}, u32[]{:S(2)}) copy-start(s32[2]{0:T(128)} %get-tuple-element.587.flags_ref) | copy-start | bytes 28
  44.7 12.4 %collective-permute-start.286 = (bf16[128,1024]{1,0:T(8,128)(2,1)S(1)}, bf16[128,1024]{1,0:T(8,128)(2,1)S(1)}, u32[]{:S(2)}, u32[]{:S(2)}) collective-permute-start(bf16[128,1024]{1,0:T(8,128)(2,1)S(1)} %get-tuple-element.607), channel_id=1, source_target_pairs={{0,8},{8,0},{16,24},{24,16},{1,9},{9,1},{17,25},{25,17},{2,10},{10... | collective-permute-start | bytes 786440 | tf_op jit(solution)/shard_map/ppermute | solution.py:19
  57.2 16.4 %copy-start = (bf16[4,128,1024]{2,1,0:T(8,128)(2,1)}, bf16[4,128,1024]{2,1,0:T(8,128)(2,1)S(1)}, u32[]{:S(2)}) copy-start(bf16[4,128,1024]{2,1,0:T(8,128)(2,1)S(1)} %join.1.mine_ref) | copy-start | bytes 3145732
  57.2 4.8 %collective-permute-start.289 = (bf16[4,128,1024]{2,1,0:T(8,128)(2,1)S(1)}, bf16[4,128,1024]{2,1,0:T(8,128)(2,1)S(1)}, u32[]{:S(2)}, u32[]{:S(2)}) collective-permute-start(bf16[4,128,1024]{2,1,0:T(8,128)(2,1)S(1)} %join.1.mine_ref), channel_id=1, source_target_pairs={{0,1},{1,0},{2,3},{3,2},{4,5},{5,4},{6,7},{7,6},{8,9},{9,8},{10,11... | collective-permute-start | bytes 3145736 | tf_op jit(solution)/shard_map/ppermute | solution.py:19
  57.6 11.9 %all-to-all-start = ((f32[32,1,640]{2,1,0:T(1,128)}), f32[32,1,640]{2,1,0:T(1,128)S(1)}, u32[]{:S(2)}, u32[]{:S(2)}) async-start(f32[32,1,640]{2,1,0:T(1,128)} %get-tuple-element.594), calls=%async_computation | async-start | bytes 163840 | tf_op jit(solution)/shard_map/all_to_all | solution.py:27
  62.0 11.6 %copy-start.2 = (bf16[4,128,1024]{2,1,0:T(8,128)(2,1)}, bf16[4,128,1024]{2,1,0:T(8,128)(2,1)S(1)}, u32[]{:S(2)}) copy-start(bf16[4,128,1024]{2,1,0:T(8,128)(2,1)S(1)} %collective-permute-done.289.got_ref) | copy-start | bytes 3145732
  62.0 2.0 %copy-start.1 = (f32[512,1024]{1,0:T(8,128)S(1)}, f32[512,1024]{1,0:T(8,128)}, u32[]{:S(2)}) copy-start(f32[512,1024]{1,0:T(8,128)} %get-tuple-element.599.scores_ref.scores_in_ref) | copy-start | bytes 6291460
  69.7 13.1 %all-to-all-start.1 = ((f32[32,1,1024]{2,1,0:T(1,128)}), f32[32,1,1024]{2,1,0:T(1,128)S(1)}, u32[]{:S(2)}, u32[]{:S(2)}) async-start(f32[32,1,1024]{2,1,0:T(1,128)} %cross.1), calls=%async_computation.1 | async-start | bytes 262144 | tf_op jit(solution)/shard_map/all_to_all | solution.py:27
  73.6 9.3 %copy-start.6 = (f32[4,128]{1,0:T(4,128)S(1)}, f32[4,128]{1,0:T(4,128)}, u32[]{:S(2)}) copy-start(f32[4,128]{1,0:T(4,128)} %log_add_fusion) | copy-start | bytes 6148
  73.6 9.3 %copy-start.7 = (f32[512]{0:T(512)S(1)}, f32[512]{0:T(512)}, u32[]{:S(2)}) copy-start(f32[512]{0:T(512)} %log_add_fusion.1) | copy-start | bytes 6148
